TPU v7x, 128 devices: a whole 4x4x4 slice. The times are simulated.
128 devices in a mesh: prow: 16 (over x, z), pcol: 8 (over y, core).
Axes of the slice: x: 4, y: 4, z: 4, core: 2. Of those that a mesh axis runs over, the one named last changes fastest.
Arguments:
- ancestor_blocks: int32 [3, 24], replicated, may hold values from -1 to 31, as said below
- root_inverse: bfloat16 [8192, 8192], P('prow', 'pcol'), may hold values from -4.5 to 4.5, as said below
- factor_rows: bfloat16 [3, 6144, 2048], P(None, 'pcol', 'prow'), may hold values from -0.078125 to 0.078125
- diag_inverse: float32 [3, 2048], P(None, 'prow'), may hold values from 0.5 to 2
Outputs:
- inverse_diagonal: float32 [3, 2048], P(None, 'prow')
Inputs may be any that keep to these rules, and one draw needn't show every extreme that they name: `ancestor_blocks`: row c lists distinct root block numbers in rising order, then -1 in the remaining slots; each child lists 24 // 2 to 24 blocks. root_inverse is exactly symmetric.
All inputs are finite; a program needn't handle non-finite values.
Results may differ from a plain program's by a relative error of at most 0.0018.
Values may be sent and summed in bfloat16 or wider, within the bound.
A program may use at most 128 MiB of HBM per device.

v0:
```python
import jax
import jax.numpy as jnp
from jax import lax
from jax.sharding import PartitionSpec as P

BLK = 256
ROOT = 8192
ROOT_BLOCKS = 32


def process(blocks, rows, diag_part, root_inverse):
    gathered = lax.all_gather(rows, "pcol", axis=1, tiled=True)
    count = gathered.shape[0]
    slots = gathered.shape[1] // BLK
    columns = gathered.shape[2]
    select = (blocks[:, :, None] == jnp.arange(ROOT_BLOCKS, dtype=jnp.int32)[None, None, :]).astype(
        jnp.bfloat16
    )
    flat = gathered.reshape(count, slots, BLK * columns)
    placed = jnp.einsum("csb,csx->cbx", select, flat, preferred_element_type=jnp.float32)
    placed = placed.astype(jnp.bfloat16).reshape(count, ROOT, columns)
    own_rows = lax.all_to_all(placed, "prow", split_axis=1, concat_axis=2, tiled=True)
    col_rows = root_inverse.shape[1]
    start = lax.axis_index("pcol") * col_rows
    local_cols = lax.dynamic_slice_in_dim(placed, start, col_rows, 1)
    partial_prod = jnp.einsum(
        "kr,ckj->crj", root_inverse, own_rows, preferred_element_type=jnp.float32
    )
    coupled = lax.psum_scatter(
        partial_prod.astype(jnp.bfloat16), "prow", scatter_dimension=2, tiled=True
    ).astype(jnp.float32)
    term = jnp.sum(local_cols.astype(jnp.float32) * coupled, axis=1)
    total = lax.psum(term, "pcol")
    return diag_part + total


def per_device(ancestor_blocks, root_inverse, factor_rows, diag_inverse):
    number = factor_rows.shape[0]
    pieces = [
        process(
            ancestor_blocks[child : child + 1],
            factor_rows[child : child + 1],
            diag_inverse[child : child + 1],
            root_inverse,
        )
        for child in range(number)
    ]
    return jnp.concatenate(pieces, axis=0)


def solution(mesh):
    in_specs = (P(), P("prow", "pcol"), P(None, "pcol", "prow"), P(None, "prow"))
    out_specs = P(None, "prow")
    return jax.shard_map(
        per_device, mesh=mesh, in_specs=in_specs, out_specs=out_specs, check_vma=False
    )
```

profile of v0, /device:TPU:1, one launch (start us, length us, event | category | flops | bytes accessed | tf_op | source)
XLA Modules:
  0.0 534.0 jit_solution(4176179193622209848)
XLA Ops:
  6.5 2.0 fusion.9
  8.6 0.0 all-gather.6.cloned.1.call-update
  8.6 0.0 all-gather.4.cloned.1.call-start
  8.7 0.7 all-gather.4.cloned.1.call-update
  9.4 0.0 all-gather.8.cloned.1.call-start
  9.4 0.7 all-gather.8.cloned.1.call-update
  10.1 0.0 reduce-scatter.6.cloned.1.call-start
  10.1 0.8 slice_bitcast_fusion.2
  10.9 26.1 %all-gather.6.cloned.1.call-done = bf16[1,6144,128]{2,1,0:T(8,128)(2,1)} async-done(((bf16[1,768,128]{2,1,0:T(8,128)(2,1)}), bf16[1,6144,128]{2,1,0:T(8,128)(2,1)}) %all-gather.6.cloned.1.call-update) | async-done | bytes 1572880 | tf_op jit(solution)/shard_map/all_gather | solution.py:12
  37.0 2.5 reshape.224
  39.6 2.2 convolution_convert_fusion.1
  41.8 2.9 reshape.225
  44.6 33.3 %copy.36 = bf16[1,8192,128]{2,0,1:T(2,128)(2,1)} copy(bf16[1,8192,128]{2,1,0:T(8,128)(2,1)S(1)} %reshape.225) | data formatting | bytes 4194304 | tf_op jit(solution)/shard_map/reshape | solution.py:21
  77.9 0.5 broadcast.85
  78.4 46.5 %reduce.4 = bf16[8192,128]{1,0:T(8,128)(2,1)} reduce(bf16[8192,1,128]{2,1,0:T(2,128)(2,1)} %bitcast.63, bf16[]{:T(256)} %broadcast.85), dimensions={1}, to_apply=%bitcast.61.reduce_sub_computation | reduce | bytes 4194306
  125.0 4.0 reshape.232
  128.9 33.9 %all_to_all.45 = bf16[16,2,32768]{2,1,0:T(2,128)(2,1)} all-to-all(bf16[16,2,32768]{2,1,0:T(2,128)(2,1)} %reshape.232), channel_id=1, replica_groups=mesh['prow'=16,'pcol'=8] {'prow'}, dimensions={0} | all-to-all | bytes 4194304 | tf_op jit(solution)/shard_map/all_to_all | solution.py:22
  162.9 10.4 %reshape.233 = bf16[8192,1,128]{2,1,0:T(2,128)(2,1)} reshape(bf16[16,2,32768]{2,1,0:T(2,128)(2,1)} %all_to_all.45) | data formatting | bytes 4194304
  173.3 3.8 copy.27
  177.1 3.9 copy.22
  181.0 5.9 %convert_bitcast_fusion.1 = bf16[1,1024,2048]{1,2,0:T(8,128)(2,1)} fusion(bf16[512,2048]{0,1:T(8,128)(2,1)} %bitcast.72, bf16[512,1024]{1,0:T(8,128)(2,1)S(1)} %copy-done), kind=kOutput, calls=%fused_computation.4 | convolution fusion | flops 2149580800 | bytes 7340032 | tf_op jit(solution)/shard_map/kr,ckj->crj/dot_general | solution.py:26
  186.9 0.0 reduce-scatter.6.cloned.1.call-update
  186.9 0.0 reduce-scatter.4.cloned.1.call-start
  186.9 0.0 all-gather.4.cloned.1.call-done
  187.0 3.7 reshape.221
  190.7 3.6 convolution_convert_fusion.2
  194.2 4.2 reshape.222
  198.5 7.5 %copy.37 = bf16[1,8192,128]{2,0,1:T(2,128)(2,1)} copy(bf16[1,8192,128]{2,1,0:T(8,128)(2,1)} %reshape.222) | data formatting | bytes 4194304 | tf_op jit(solution)/shard_map/reshape | solution.py:21
  205.9 46.6 %reduce.5 = bf16[8192,128]{1,0:T(8,128)(2,1)} reduce(bf16[8192,1,128]{2,1,0:T(2,128)(2,1)} %bitcast.68, bf16[]{:T(256)} %broadcast.85), dimensions={1}, to_apply=%bitcast.62.reduce_sub_computation | reduce | bytes 4194306
  252.5 4.0 reshape.234
  256.5 30.7 %all_to_all.46 = bf16[16,2,32768]{2,1,0:T(2,128)(2,1)} all-to-all(bf16[16,2,32768]{2,1,0:T(2,128)(2,1)} %reshape.234), channel_id=1, replica_groups=mesh['prow'=16,'pcol'=8] {'prow'}, dimensions={0} | all-to-all | bytes 4194304 | tf_op jit(solution)/shard_map/all_to_all | solution.py:22
  287.2 10.5 %reshape.235 = bf16[8192,1,128]{2,1,0:T(2,128)(2,1)} reshape(bf16[16,2,32768]{2,1,0:T(2,128)(2,1)} %all_to_all.46) | data formatting | bytes 4194304
  297.6 3.9 copy.26
  301.5 3.9 copy.19
  305.4 5.9 %convert_bitcast_fusion.2 = bf16[1,1024,2048]{1,2,0:T(8,128)(2,1)} fusion(bf16[512,2048]{0,1:T(8,128)(2,1)} %bitcast.73, bf16[512,1024]{1,0:T(8,128)(2,1)S(1)} %copy-done), kind=kOutput, calls=%fused_computation.5 | convolution fusion | flops 2149580800 | bytes 7340032 | tf_op jit(solution)/shard_map/kr,ckj->crj/dot_general | solution.py:26
  311.3 0.0 reduce-scatter.4.cloned.1.call-update
  311.3 0.0 reduce-scatter.8.cloned.1.call-start
  311.4 0.0 all-gather.8.cloned.1.call-done
  311.4 3.7 reshape.227
  315.1 3.6 convolution_convert_fusion
  318.7 4.2 reshape.228
  322.9 7.5 %copy.35 = bf16[1,8192,128]{2,0,1:T(2,128)(2,1)} copy(bf16[1,8192,128]{2,1,0:T(8,128)(2,1)} %reshape.228) | data formatting | bytes 4194304 | tf_op jit(solution)/shard_map/reshape | solution.py:21
  330.5 46.6 %reduce.3 = bf16[8192,128]{1,0:T(8,128)(2,1)} reduce(bf16[8192,1,128]{2,1,0:T(2,128)(2,1)} %bitcast.66, bf16[]{:T(256)} %broadcast.85), dimensions={1}, to_apply=%bitcast.60.reduce_sub_computation | reduce | bytes 4194306
  377.1 4.0 reshape.230
  381.1 28.7 %all_to_all.47 = bf16[16,2,32768]{2,1,0:T(2,128)(2,1)} all-to-all(bf16[16,2,32768]{2,1,0:T(2,128)(2,1)} %reshape.230), channel_id=1, replica_groups=mesh['prow'=16,'pcol'=8] {'prow'}, dimensions={0} | all-to-all | bytes 4194304 | tf_op jit(solution)/shard_map/all_to_all | solution.py:22
  409.7 10.5 %reshape.231 = bf16[8192,1,128]{2,1,0:T(2,128)(2,1)} reshape(bf16[16,2,32768]{2,1,0:T(2,128)(2,1)} %all_to_all.47) | data formatting | bytes 4194304
  420.2 3.8 copy.28
  424.0 3.9 copy.25
  428.0 5.9 %convert_bitcast_fusion = bf16[1,1024,2048]{1,2,0:T(8,128)(2,1)} fusion(bf16[512,2048]{0,1:T(8,128)(2,1)} %bitcast.74, bf16[512,1024]{1,0:T(8,128)(2,1)S(1)} %copy-done), kind=kOutput, calls=%fused_computation.3 | convolution fusion | flops 2149580800 | bytes 7340032 | tf_op jit(solution)/shard_map/kr,ckj->crj/dot_general | solution.py:26
  433.9 0.0 reduce-scatter.8.cloned.1.call-update
  433.9 0.0 copy-start.1
  433.9 0.1 copy.30
  434.1 1.0 constant_dynamic-slice_fusion.2
  435.1 0.1 copy.29
  435.2 1.0 constant_dynamic-slice_fusion
  436.2 0.1 copy.31
  436.3 0.0 reduce-scatter.6.cloned.1.call-done
  436.4 1.1 multiply_reduce_fusion.1
  437.5 0.0 reduce-scatter.4.cloned.1.call-done
  437.5 1.1 multiply_reduce_fusion.2
  438.6 72.8 %reduce-scatter.8.cloned.1.call-done = bf16[1,1024,128]{1,2,0:T(8,128)(2,1)} async-done(((bf16[1,1024,2048]{1,2,0:T(8,128)(2,1)}), bf16[1,1024,128]{1,2,0:T(8,128)(2,1)}) %reduce-scatter.8.cloned.1.call-update) | async-done | bytes 262160 | tf_op jit(solution)/shard_map/reduce_scatter | solution.py:29
  511.4 1.1 multiply_reduce_fusion
  512.5 14.1 %all-reduce = (f32[1,128]{1,0:T(1,128)S(1)}, f32[1,128]{1,0:T(1,128)S(1)}, f32[1,128]{1,0:T(1,128)S(1)}) all-reduce(f32[1,128]{1,0:T(1,128)S(1)} %bitcast.77, f32[1,128]{1,0:T(1,128)S(1)} %bitcast.75, f32[1,128]{1,0:T(1,128)S(1)} %bitcast.76), channel_id=1, replica_groups=mesh['prow'=16,'pcol'=8] {'pcol'}, use_global_device_ids=true, to_apply=%region_8.0 | all-reduce | flops 384 | bytes 3072 | tf_op jit(solution)/shard_map/psum | solution.py:33
  526.6 0.6 pad_maximum_fusion
  (6 shorter events, 0.0 us)
Async XLA Ops:
  6.5 174.5 %copy-start = (bf16[512,1024]{1,0:T(8,128)(2,1)S(1)}, bf16[512,1024]{1,0:T(8,128)(2,1)}, u32[]{:S(2)}) copy-start(bf16[512,1024]{1,0:T(8,128)(2,1)} %param.5) | copy-start | bytes 3145732
  6.5 30.5 %all-gather.6.cloned.1.call-start = ((), (), s32[]{:S(2)}) async-start(), calls=%async_computation.8 | async-start | bytes 1769472 | tf_op jit(solution)/shard_map/all_gather | solution.py:12
  8.6 178.4 %all-gather.4.cloned.1.call-start = ((), (), s32[]{:S(2)}) async-start(), calls=%async_computation.6 | async-start | bytes 1769472 | tf_op jit(solution)/shard_map/all_gather | solution.py:12
  9.4 302.0 %all-gather.8.cloned.1.call-start = ((), (), s32[]{:S(2)}) async-start(), calls=%async_computation.10 | async-start | bytes 1769472 | tf_op jit(solution)/shard_map/all_gather | solution.py:12
  10.1 426.3 %reduce-scatter.6.cloned.1.call-start = ((), (), s32[]{:S(2)}) async-start(), calls=%async_computation.9 | async-start | bytes 4456448 | tf_op jit(solution)/shard_map/reduce_scatter | solution.py:29
  186.9 250.6 %reduce-scatter.4.cloned.1.call-start = ((), (), s32[]{:S(2)}) async-start(), calls=%async_computation.7 | async-start | bytes 4456448 | tf_op jit(solution)/shard_map/reduce_scatter | solution.py:29
  311.3 200.0 %reduce-scatter.8.cloned.1.call-start = ((), (), s32[]{:S(2)}) async-start(), calls=%async_computation.11 | async-start | bytes 4456448 | tf_op jit(solution)/shard_map/reduce_scatter | solution.py:29
  433.9 92.7 %copy-start.1 = (f32[3,128]{1,0:T(4,128)S(1)}, f32[3,128]{1,0:T(4,128)}, u32[]{:S(2)}) copy-start(f32[3,128]{1,0:T(4,128)} %param.7) | copy-start | bytes 4612
Sparse Core Ops, SparseCore 0:
  9.0 27.9 all-gather.5
  38.7 24.5 all-gather.3
  65.0 24.5 all-gather.7
  187.0 74.2 reduce-scatter.5
  311.5 75.3 reduce-scatter.3
  434.0 77.3 reduce-scatter.7
where the time goes:
time: 537 us; the launch traced here: 534 us
  other arithmetic  144 us (27%)
  local copies, waits for them, and re-layouts  142 us (26%)
  blocking collectives  107 us (20%)
  waiting for transfers between devices  100 us (19%)
  matrix products  27 us (5%)
  between operations  13.6 us (3%)
    unnamed x3, other arithmetic  140 us
    all_to_all x3, blocking collectives, process(): lax.all_to_all(placed, 'prow', split_axis=1, concat_axis=2, tiled=True)  93.3 us
    reduce_scatter x3, waiting for transfers between devices, process(): lax.psum_scatter(partial_prod.astype(jnp.bfloat16), 'prow', scatter_dimen...  72.8 us
    reshape x6, local copies, waits for them, and re-layouts, process(): placed = placed.astype(jnp.bfloat16).reshape(count, ROOT, columns)  59.6 us
    unnamed x17, local copies, waits for them, and re-layouts  55.8 us
    all_gather x3, waiting for transfers between devices, process(): gathered = lax.all_gather(rows, 'pcol', axis=1, tiled=True)  26.1 us
    dot_general x3, matrix products, process(): jnp.einsum('kr,ckj->crj', root_inverse, own_rows, preferred_element_type=...  17.7 us
    psum x1, blocking collectives, process(): total = lax.psum(term, 'pcol')  14.1 us
  transfers between devices with their start and end apart: 6, of which 2 were waited for; matrix products, arithmetic and copies ran while one was open for 58% of the time, Pallas kernels for 0%

commit v1 on v0

v1 whole, which is shorter than its diff:
```python
import jax
import jax.numpy as jnp
from jax import lax
from jax.experimental import pallas as pl
from jax.experimental.pallas import tpu as pltpu
from jax.sharding import PartitionSpec as P

MESH = pl.DeviceIdType.MESH
BLK = 256
CHILDREN = 3
ROOT_BLOCKS = 32
MAX_ANC = 24
Z_FIRST = (1, 2, 2)
FAR_UP = (1, 1, 0)
SOURCES = ((0, 0), (0, 1), (1, 0), (3, 0), (1, 1), (3, 1), (2, 0), (2, 1))
UNITS = 2 * len(SOURCES)
COPIES = 96


def pick(index, values):
    out = jnp.int32(values[0])
    for at, value in enumerate(values[1:], 1):
        out = jnp.where(index == at, jnp.int32(value), out)
    return out


def kernel(
    anc,
    root,
    rows,
    out,
    pb0,
    pb1,
    pb2,
    rb,
    ext,
    pk0,
    pk1,
    pk2,
    acc,
    part,
    red,
    slot_of,
    listed,
    unit_row,
    unit_win,
    local_sem,
    send_sem,
    recv_sem,
    ext_send,
    ext_recv,
    red_send,
    red_recv,
):
    pb, pk = (pb0, pb1, pb2), (pk0, pk1, pk2)
    p, q = lax.axis_index("prow"), lax.axis_index("pcol")
    x, z = p // 4, p % 4
    y, core = q // 2, q % 2
    zp = z + 1 - 2 * (z % 2)
    zq = (z + 3 + 2 * (z % 2)) % 4
    up, down, far = (y + 1) % 4, (y + 3) % 4, (y + 2) % 4

    def device(px, py, pz, pc):
        return (px * 4 + pz, py * 2 + pc)

    d_z = device(x, y, zp, core)
    d_yu, d_yd = device(x, up, z, core), device(x, down, z, core)
    d_zq = device(x, y, zq, core)
    d_xu, d_xd = device((x + 1) % 4, y, z, core), device((x + 3) % 4, y, z, core)
    d_core = device(x, y, z, 1 - core)

    def window(px, pz, t):
        diagonal = jnp.logical_and(px == y, pz // 2 == core)
        second = pz - 2 * core
        below = px * 4 + pz < 2 * q
        plain = 1 + 2 * jnp.where(below, t, 1 - t)
        special = jnp.where(second == 0, 1, 2) if t == 0 else jnp.where(second == 0, 3, 0)
        return jnp.where(diagonal, special, plain).astype(jnp.int32)

    own_diag = jnp.logical_and(x == y, z // 2 == core)
    z_ext = jnp.where(z // 2 == core, z, zq)
    ext_key = 1 + (z_ext - 2 * core)
    ext_row = 2 * (4 * y + z_ext) + 1

    local = []
    for c in range(CHILDREN):
        local.append(
            pltpu.make_async_copy(
                rows.at[c], pb[c].at[0, y, pl.ds(core * 3, 3)], local_sem.at[c]
            )
        )
    for t in range(2):
        win = window(x, z, t)
        for h, values in enumerate(((3, 0, 2, 1), (0, 2, 1, 3))):
            column = pl.multiple_of(pick(win, values) * BLK, BLK)
            local.append(
                pltpu.make_async_copy(
                    root.at[pl.ds(t * BLK, BLK), pl.ds(column, BLK)],
                    rb.at[t, :, pl.ds(h * BLK, BLK)],
                    local_sem.at[3 + 2 * t + h],
                )
            )
    ext_column = pl.multiple_of(jnp.where(z - 2 * core == 1, 2 * BLK, 0), BLK)
    local_ext = pltpu.make_async_copy(
        root.at[pl.ds(BLK, BLK), pl.ds(ext_column, BLK)], ext, local_sem.at[7]
    )
    for copy in local:
        copy.start()

    @pl.when(own_diag)
    def _():
        local_ext.start()

    group = [(dy, dc, dz) for dy in range(4) for dc in range(2) for dz in range(2)][1:]

    def member(dy, dc, dz):
        return device(x, (y + dy) % 4, zp if dz else z, 1 - core if dc else core)

    partners = [member(*g) for g in group] + [d_zq, d_xu, d_xd]
    barrier = pltpu.get_barrier_semaphore()
    for partner in partners:
        pl.semaphore_signal(barrier, inc=1, device_id=partner, device_id_type=MESH)
    for copy in local:
        copy.wait()

    @pl.when(own_diag)
    def _():
        local_ext.wait()
        for t in range(2):
            rb[t, :, 0:BLK] = rb[t, :, 0:BLK] * jnp.bfloat16(0.5)

    pl.semaphore_wait(barrier, len(partners))

    sent = []

    def send(src, dst, target):
        n = len(sent)
        copy = pltpu.make_async_remote_copy(
            src_ref=src,
            dst_ref=dst,
            send_sem=send_sem.at[n],
            recv_sem=recv_sem.at[n],
            device_id=target,
            device_id_type=MESH,
        )
        copy.start()
        sent.append(copy)
        return copy

    def slots(c, zz, py, lo, hi):
        return pb[c].at[zz, py, pl.ds(core * 3 + lo, hi - lo)]

    def unit(dx, zr, t):
        return rb.at[2 * SOURCES.index((dx, zr)) + t]

    def p_a(c):
        return send(slots(c, 0, y, 0, 3), slots(c, 1, y, 0, 3), d_z)

    def p_b(c):
        own = slots(c, 0, y, 0, 3)
        return send(own, own, d_yu), send(own, own, d_yd)

    def p_c(c):
        ref = slots(c, 1, y, 0, Z_FIRST[c])
        return send(ref, ref, d_yu), send(ref, ref, d_yd)

    def p_d_up(c):
        ref = slots(c, 0, down, 0, Z_FIRST[c] + FAR_UP[c])
        return send(ref, ref, d_yu)

    def p_d_down(c):
        if Z_FIRST[c] + FAR_UP[c] == 3:
            return None
        ref = slots(c, 0, up, Z_FIRST[c] + FAR_UP[c], 3)
        return send(ref, ref, d_yd)

    def p_d_other(c):
        ref = slots(c, 1, up, 0, Z_FIRST[c])
        return send(ref, ref, d_yd)

    def p_e(c, py):
        return send(slots(c, 0, py, Z_FIRST[c], 3), slots(c, 1, py, Z_FIRST[c], 3), d_z)

    def p_core(c, zz, py, lo, hi):
        ref = slots(c, zz, py, lo, hi)
        return send(ref, ref, d_core)

    def p_core_all(c):
        ref = pb[c].at[:, :, pl.ds(core * 3, 3)]
        return send(ref, ref, d_core)

    a, b, cc, du, dd, do, e = {}, {}, {}, {}, {}, {}, {}
    kids = []
    a[0] = p_a(0)
    b[0] = p_b(0)
    r_a0 = send(unit(0, 0, 0), unit(0, 1, 0), d_zq)
    r_b1 = send(unit(0, 0, 1), unit(3, 0, 1), d_xu), send(unit(0, 0, 1), unit(1, 0, 1), d_xd)
    r_a1 = send(unit(0, 0, 1), unit(0, 1, 1), d_zq)
    r_b0 = send(unit(0, 0, 0), unit(3, 0, 0), d_xu), send(unit(0, 0, 0), unit(1, 0, 0), d_xd)
    a[1] = p_a(1)
    b[1] = p_b(1)

    ext_is_mine = z_ext == z
    dx_ext = (x - y + 4) % 4

    def ext_copy(n, target):
        return pltpu.make_async_remote_copy(
            src_ref=ext,
            dst_ref=ext,
            send_sem=ext_send.at[n],
            recv_sem=ext_recv,
            device_id=target,
            device_id_type=MESH,
        )

    to_zq, to_xu, to_xd = ext_copy(0, d_zq), ext_copy(1, d_xu), ext_copy(2, d_xd)
    goes_zq = ext_is_mine
    goes_xu = jnp.logical_and(ext_is_mine, jnp.logical_or(dx_ext == 0, dx_ext == 1))
    goes_xd = jnp.logical_and(ext_is_mine, dx_ext == 0)

    def ext_forward():
        @pl.when(jnp.logical_not(own_diag))
        def _():
            to_zq.wait_recv()

        @pl.when(goes_xu)
        def _():
            to_xu.start()

        @pl.when(goes_xd)
        def _():
            to_xd.start()

        @pl.when(goes_zq)
        def _():
            to_zq.start()

    for c in range(CHILDREN):

        def find(block, at, c=c):
            hit = (anc[c, at] == block).astype(jnp.int32)
            slot_of[c, block] = at
            listed[c, block] = hit.astype(jnp.float32)
            return jnp.minimum(at + hit, MAX_ANC - 1)

        lax.fori_loop(0, ROOT_BLOCKS, find, jnp.int32(0))
    for at, (dx, zr) in enumerate(SOURCES):
        px, pz = (x + dx) % 4, zq if zr else z
        for t in range(2):
            unit_row[2 * at + t] = 2 * (px * 4 + pz) + t
            unit_win[2 * at + t] = window(px, pz, t)
    acc[...] = jnp.zeros_like(acc)
    part[...] = jnp.zeros_like(part)

    def build(c):
        for at, key in enumerate((3, 0, 2, 1, 3)):
            block = 4 * q + key
            slot, keep = slot_of[c, block], listed[c, block].astype(jnp.bfloat16)
            for zz in range(2):
                pk[c][at * BLK : (at + 1) * BLK, zz * 128 : (zz + 1) * 128] = (
                    pb[c][zz, slot // 6, slot % 6] * keep
                )

    def add(c, product, row):
        slot, keep = slot_of[c, row], listed[c, row]
        for zz in range(2):
            mine = pb[c][zz, slot // 6, slot % 6].astype(jnp.float32)
            term = product[:, zz * 128 : (zz + 1) * 128] * mine
            acc[c, zz] += jnp.sum(term.reshape(BLK // 8, 8, 128), axis=0) * keep

    def compute(c, lo, hi):
        def step(u, carry):
            start = pl.multiple_of(unit_win[u] * BLK, BLK)
            product = jnp.dot(
                rb[u], pk[c][pl.ds(start, 2 * BLK), :], preferred_element_type=jnp.float32
            )
            add(c, product, unit_row[u])
            return carry

        lax.fori_loop(lo, hi, step, 0)

    def compute_ext(c):
        start = pl.multiple_of(ext_key * BLK, BLK)
        product = jnp.dot(
            ext[...], pk[c][pl.ds(start, BLK), :], preferred_element_type=jnp.float32
        )
        add(c, product, ext_row)

    def after_b(c):
        b[c][0].wait_recv()
        b[c][1].wait_recv()
        du[c] = p_d_up(c)
        dd[c] = p_d_down(c)
        e[c] = [p_e(c, down), p_e(c, up)]

    def after_a(c):
        a[c].wait_recv()
        cc[c] = p_c(c)

    def after_c(c):
        cc[c][0].wait_recv()
        cc[c][1].wait_recv()
        do[c] = p_d_other(c)

    def after_d(c):
        du[c].wait_recv()
        if dd[c] is not None:
            dd[c].wait_recv()
        e[c].append(p_e(c, far))

    after_a(0)
    after_b(0)
    r_a0.wait_recv()
    r_c0 = send(unit(0, 1, 0), unit(3, 1, 0), d_xu), send(unit(0, 1, 0), unit(1, 1, 0), d_xd)
    r_b1[0].wait_recv()
    r_b1[1].wait_recv()
    half = BLK // 2
    r_d1 = (
        send(unit(3, 0, 1).at[pl.ds(0, half)], unit(2, 0, 1).at[pl.ds(0, half)], d_xu),
        send(unit(1, 0, 1).at[pl.ds(half, half)], unit(2, 0, 1).at[pl.ds(half, half)], d_xd),
    )
    r_e1 = [send(unit(3, 0, 1), unit(3, 1, 1), d_zq), send(unit(1, 0, 1), unit(1, 1, 1), d_zq)]
    ext_forward()
    after_c(0)
    a[2] = p_a(2)
    b[2] = p_b(2)
    after_a(1)
    after_b(1)
    after_d(0)
    r_b0[0].wait_recv()
    r_b0[1].wait_recv()
    r_d0u = send(unit(3, 0, 0), unit(2, 0, 0), d_xu)
    r_a1.wait_recv()
    r_d1[0].wait_recv()
    r_d1[1].wait_recv()
    r_e1.append(send(unit(2, 0, 1), unit(2, 1, 1), d_zq))
    after_c(1)
    r_c0[0].wait_recv()
    r_c0[1].wait_recv()
    r_d0d = send(unit(1, 1, 0), unit(2, 1, 0), d_xd)
    after_a(2)
    after_b(2)
    after_d(1)
    do[0].wait_recv()
    for copy in e[0]:
        copy.wait_recv()
    kids.append(p_core_all(0))
    late = [p_core(2, 0, y, 0, 3), p_core(2, 0, up, 0, 3), p_core(2, 0, down, 0, 3), p_core(2, 1, y, 0, 3)]
    after_c(2)
    kids[0].wait_recv()
    build(0)
    compute(0, 0, 8)
    after_d(2)
    late.append(p_core(2, 0, far, 0, 3))
    compute_ext(0)
    r_e1[0].wait_recv()
    r_e1[1].wait_recv()
    compute(0, 8, 12)
    do[1].wait_recv()
    for copy in e[1]:
        copy.wait_recv()
    kids.append(p_core_all(1))
    r_d0u.wait_recv()
    compute(0, 12, 14)
    kids[1].wait_recv()
    build(1)
    compute(1, 0, 14)
    compute_ext(1)
    r_d0d.wait_recv()
    r_e1[2].wait_recv()
    compute(0, 14, 16)
    compute(1, 14, 16)
    do[2].wait_recv()
    for copy in e[2]:
        copy.wait_recv()
    for py in (down, up, far):
        late.append(p_core(2, 1, py, 0, 3))
    for copy in late:
        copy.wait_recv()
    build(2)
    compute(2, 0, UNITS)
    compute_ext(2)

    for zz in range(2):
        for c in range(CHILDREN):
            part[zz, c : c + 1, :] = 2.0 * jnp.sum(acc[c, zz], axis=0, keepdims=True)
    mine = q * 2 + z % 2
    sums = []
    for n, g in enumerate(group):
        copy = pltpu.make_async_remote_copy(
            src_ref=part.at[g[2]],
            dst_ref=red.at[mine],
            send_sem=red_send.at[n],
            recv_sem=red_recv.at[n],
            device_id=member(*g),
            device_id_type=MESH,
        )
        copy.start()
        sums.append(copy)
    red[mine] = part[0]
    for copy in sent:
        copy.wait_send()

    @pl.when(goes_zq)
    def _():
        to_zq.wait_send()

    @pl.when(goes_xu)
    def _():
        to_xu.wait_send()

    @pl.when(goes_xd)
    def _():
        to_xd.wait_send()

    for copy in sums:
        copy.wait()
    total = red[0]
    for at in range(1, 16):
        total = total + red[at]
    out[...] = total


def per_device(ancestor_blocks, root_inverse, factor_rows, diag_inverse):
    vmem, smem, dma = pltpu.VMEM, pltpu.SMEM, pltpu.SemaphoreType.DMA
    rows = factor_rows.reshape(CHILDREN, 3, BLK, 128)
    total = pl.pallas_call(
        kernel,
        out_shape=jax.ShapeDtypeStruct((8, 128), jnp.float32),
        in_specs=[
            pl.BlockSpec(memory_space=smem),
            pl.BlockSpec(memory_space=pl.ANY),
            pl.BlockSpec(memory_space=pl.ANY),
        ],
        out_specs=pl.BlockSpec(memory_space=vmem),
        scratch_shapes=[vmem((2, 4, 6, BLK, 128), jnp.bfloat16)] * CHILDREN
        + [
            vmem((UNITS, BLK, 2 * BLK), jnp.bfloat16),
            vmem((BLK, BLK), jnp.bfloat16),
        ]
        + [vmem((5 * BLK, 2 * 128), jnp.bfloat16)] * CHILDREN
        + [
            vmem((CHILDREN, 2, 8, 128), jnp.float32),
            vmem((2, 8, 128), jnp.float32),
            vmem((16, 8, 128), jnp.float32),
            smem((CHILDREN, ROOT_BLOCKS), jnp.int32),
            smem((CHILDREN, ROOT_BLOCKS), jnp.float32),
            smem((UNITS,), jnp.int32),
            smem((UNITS,), jnp.int32),
            dma((8,)),
            dma((COPIES,)),
            dma((COPIES,)),
            dma((3,)),
            dma,
            dma((15,)),
            dma((15,)),
        ],
        compiler_params=pltpu.CompilerParams(
            collective_id=0, has_side_effects=True, vmem_limit_bytes=40 * 2**20
        ),
    )(ancestor_blocks, root_inverse, rows)
    return diag_inverse + total[:CHILDREN]


def solution(mesh):
    in_specs = (P(), P("prow", "pcol"), P(None, "pcol", "prow"), P(None, "prow"))
    out_specs = P(None, "prow")
    return jax.shard_map(
        per_device, mesh=mesh, in_specs=in_specs, out_specs=out_specs, check_vma=False
    )
```

time: 537 us -> 81.5 us (0.15)
  other arithmetic: 144 us -> 0.58 us
  local copies, waits for them, and re-layouts: 142 us -> 2.97 us
  blocking collectives: 107 us -> 0 us
  waiting for transfers between devices: 100 us -> 0 us
  Pallas kernels: 0 us -> 77.7 us
  matrix products: 27 us -> 0 us
  between operations: 13.6 us -> 0.02 us
    unnamed x3 -> x0, other arithmetic: 140 us -> none
    all_to_all x3 -> x0, blocking collectives: 93.3 us -> none  [process(): lax.all_to_all(placed, 'prow', split_axis=1, concat_axis=2, tiled=True)]
    pallas_call x0 -> x1, Pallas kernels: none -> 77.7 us  [per_device(): pl.pallas_call(kernel, out_shape=jax.ShapeDtypeStruct((8, 128), jnp.float...]
    reduce_scatter x3 -> x0, waiting for transfers between devices: 72.8 us -> none  [process(): lax.psum_scatter(partial_prod.astype(jnp.bfloat16), 'prow', scatter_dimen...]
    reshape x6 -> x0, local copies, waits for them, and re-layouts: 59.6 us -> none  [process(): placed = placed.astype(jnp.bfloat16).reshape(count, ROOT, columns)]
    unnamed x17 -> x8, local copies, waits for them, and re-layouts: 55.8 us -> 2.97 us
    dot_general x6 -> x0, matrix products: 27 us -> none  [the longest x3 17.7 us: process(): jnp.einsum('kr,ckj->crj', root_inverse, own_rows, preferred_element_type=...]
    all_gather x3 -> x0, waiting for transfers between devices: 26.1 us -> none  [process(): gathered = lax.all_gather(rows, 'pcol', axis=1, tiled=True)]
  transfers between devices with their start and end apart: 6 -> 0, of which waited for: 2 -> 0; matrix products, arithmetic and copies ran while one was open for 58% -> 0% of each run, Pallas kernels for 0% -> 0%
where the time goes in v1:
time: 81.5 us; the launch traced here: 81.3 us
  Pallas kernels  77.7 us (95%)
  local copies, waits for them, and re-layouts  2.97 us (4%)
    pallas_call x1, Pallas kernels, per_device(): pl.pallas_call(kernel, out_shape=jax.ShapeDtypeStruct((8, 128), jnp.float...  77.7 us
    unnamed x8, local copies, waits for them, and re-layouts  2.97 us

profile of v1, /device:TPU:1, one launch (start us, length us, event | category | flops | bytes accessed | tf_op | source)
XLA Modules:
  0.0 81.3 jit_solution(294200366149506473)
XLA Ops:
  0.0 0.0 copy-start
  0.0 1.2 %copy-done = bf16[512,1024]{1,0:T(8,128)(2,1)S(1)} copy-done((bf16[512,1024]{1,0:T(8,128)(2,1)S(1)}, bf16[512,1024]{1,0:T(8,128)(2,1)}, u32[]{:S(2)}) %copy-start) | copy-done | bytes 1048600
  1.2 0.0 copy-start.1
  1.2 1.1 %copy-done.1 = bf16[3,768,128]{2,1,0:T(8,128)(2,1)S(1)} copy-done((bf16[3,768,128]{2,1,0:T(8,128)(2,1)S(1)}, bf16[3,768,128]{2,1,0:T(8,128)(2,1)}, u32[]{:S(2)}) %copy-start.1) | copy-done | bytes 589848
  2.3 0.0 copy-start.2
  2.3 0.7 copy-done.2
  3.0 0.0 copy-start.3
  3.0 77.7 %shard_map.46 = f32[8,128]{1,0:T(8,128)S(1)} custom-call(s32[3,24]{1,0:T(4,128)S(1)} %copy-done.2, bf16[512,1024]{1,0:T(8,128)(2,1)S(1)} %copy-done, bf16[3,3,256,128]{3,2,1,0:T(8,128)(2,1)S(1)} %bitcast.1), custom_call_target="tpu_custom_call" | custom-call | tf_op jit(solution)/shard_map/pallas_call | solution.py:427
  80.7 0.0 copy-done.3
  80.7 0.6 slice_add_fusion
Async XLA Ops:
  0.0 1.2 %copy-start = (bf16[512,1024]{1,0:T(8,128)(2,1)S(1)}, bf16[512,1024]{1,0:T(8,128)(2,1)}, u32[]{:S(2)}) copy-start(bf16[512,1024]{1,0:T(8,128)(2,1)} %root.1) | copy-start | bytes 3145732
  1.2 1.1 %copy-start.1 = (bf16[3,768,128]{2,1,0:T(8,128)(2,1)S(1)}, bf16[3,768,128]{2,1,0:T(8,128)(2,1)}, u32[]{:S(2)}) copy-start(bf16[3,768,128]{2,1,0:T(8,128)(2,1)} %param.6) | copy-start | bytes 1769476
  2.3 0.7 copy-start.2
  3.0 77.7 %copy-start.3 = (f32[3,128]{1,0:T(4,128)S(1)}, f32[3,128]{1,0:T(4,128)}, u32[]{:S(2)}) copy-start(f32[3,128]{1,0:T(4,128)} %param.7) | copy-start | bytes 4612

commit v2 on v1

--- a/solution.py
+++ b/solution.py
@@ -189,6 +189,48 @@
         ref = pb[c].at[:, :, pl.ds(core * 3, 3)]
         return send(ref, ref, d_core)
 
+    ext_is_mine = z_ext == z
+    dx_ext = (x - y + 4) % 4
+
+    def ext_copy(n, target):
+        return pltpu.make_async_remote_copy(
+            src_ref=ext,
+            dst_ref=ext,
+            send_sem=ext_send.at[n],
+            recv_sem=ext_recv,
+            device_id=target,
+            device_id_type=MESH,
+        )
+
+    to_zq, to_xu, to_xd = ext_copy(0, d_zq), ext_copy(1, d_xu), ext_copy(2, d_xd)
+    goes_zq = ext_is_mine
+    goes_xu = jnp.logical_and(ext_is_mine, jnp.logical_or(dx_ext == 0, dx_ext == 1))
+    goes_xd = jnp.logical_and(ext_is_mine, dx_ext == 0)
+
+    near = jnp.logical_and(ext_is_mine, dx_ext % 2 == 1)
+    opposite = jnp.logical_and(ext_is_mine, dx_ext == 2)
+
+    def ext_on(here, more):
+        @pl.when(here)
+        def _():
+            to_zq.wait_recv()
+
+        if more:
+
+            @pl.when(jnp.logical_and(here, dx_ext == 1))
+            def _():
+                to_xu.start()
+
+        @pl.when(here)
+        def _():
+            to_zq.start()
+
+    @pl.when(own_diag)
+    def _():
+        to_xu.start()
+        to_xd.start()
+        to_zq.start()
+
     a, b, cc, du, dd, do, e = {}, {}, {}, {}, {}, {}, {}
     kids = []
     a[0] = p_a(0)
@@ -199,41 +241,6 @@
     r_b0 = send(unit(0, 0, 0), unit(3, 0, 0), d_xu), send(unit(0, 0, 0), unit(1, 0, 0), d_xd)
     a[1] = p_a(1)
     b[1] = p_b(1)
-
-    ext_is_mine = z_ext == z
-    dx_ext = (x - y + 4) % 4
-
-    def ext_copy(n, target):
-        return pltpu.make_async_remote_copy(
-            src_ref=ext,
-            dst_ref=ext,
-            send_sem=ext_send.at[n],
-            recv_sem=ext_recv,
-            device_id=target,
-            device_id_type=MESH,
-        )
-
-    to_zq, to_xu, to_xd = ext_copy(0, d_zq), ext_copy(1, d_xu), ext_copy(2, d_xd)
-    goes_zq = ext_is_mine
-    goes_xu = jnp.logical_and(ext_is_mine, jnp.logical_or(dx_ext == 0, dx_ext == 1))
-    goes_xd = jnp.logical_and(ext_is_mine, dx_ext == 0)
-
-    def ext_forward():
-        @pl.when(jnp.logical_not(own_diag))
-        def _():
-            to_zq.wait_recv()
-
-        @pl.when(goes_xu)
-        def _():
-            to_xu.start()
-
-        @pl.when(goes_xd)
-        def _():
-            to_xd.start()
-
-        @pl.when(goes_zq)
-        def _():
-            to_zq.start()
 
     for c in range(CHILDREN):
 
@@ -320,7 +327,7 @@
         send(unit(1, 0, 1).at[pl.ds(half, half)], unit(2, 0, 1).at[pl.ds(half, half)], d_xd),
     )
     r_e1 = [send(unit(3, 0, 1), unit(3, 1, 1), d_zq), send(unit(1, 0, 1), unit(1, 1, 1), d_zq)]
-    ext_forward()
+    ext_on(near, True)
     after_c(0)
     a[2] = p_a(2)
     b[2] = p_b(2)
@@ -345,6 +352,7 @@
     for copy in e[0]:
         copy.wait_recv()
     kids.append(p_core_all(0))
+    ext_on(opposite, False)
     late = [p_core(2, 0, y, 0, 3), p_core(2, 0, up, 0, 3), p_core(2, 0, down, 0, 3), p_core(2, 1, y, 0, 3)]
     after_c(2)
     kids[0].wait_recv()
@@ -352,7 +360,6 @@
     compute(0, 0, 8)
     after_d(2)
     late.append(p_core(2, 0, far, 0, 3))
-    compute_ext(0)
     r_e1[0].wait_recv()
     r_e1[1].wait_recv()
     compute(0, 8, 12)
@@ -365,7 +372,6 @@
     kids[1].wait_recv()
     build(1)
     compute(1, 0, 14)
-    compute_ext(1)
     r_d0d.wait_recv()
     r_e1[2].wait_recv()
     compute(0, 14, 16)
@@ -379,7 +385,13 @@
         copy.wait_recv()
     build(2)
     compute(2, 0, UNITS)
-    compute_ext(2)
+
+    @pl.when(jnp.logical_not(ext_is_mine))
+    def _():
+        to_zq.wait_recv()
+
+    for c in range(CHILDREN):
+        compute_ext(c)
 
     for zz in range(2):
         for c in range(CHILDREN):
@@ -456,7 +468,7 @@
             dma((15,)),
         ],
         compiler_params=pltpu.CompilerParams(
-            collective_id=0, has_side_effects=True, vmem_limit_bytes=40 * 2**20
+            collective_id=0, has_side_effects=True, vmem_limit_bytes=62 * 2**20
         ),
     )(ancestor_blocks, root_inverse, rows)
     return diag_inverse + total[:CHILDREN]

time: 81.5 us -> 64.5 us (0.79)
  Pallas kernels: 77.7 us -> 63 us
  local copies, waits for them, and re-layouts: 2.97 us -> 0.01 us
    pallas_call x1, Pallas kernels: 77.7 us -> 63 us  [per_device(): pl.pallas_call(kernel, out_shape=jax.ShapeDtypeStruct((8, 128), jnp.float...]
    unnamed x8 -> x2, local copies, waits for them, and re-layouts: 2.97 us -> 0.01 us
where the time goes in v2:
time: 64.5 us; the launch traced here: 64.3 us
  Pallas kernels  63 us (98%)
  other arithmetic  1.25 us (2%)
    pallas_call x1, Pallas kernels, per_device(): pl.pallas_call(kernel, out_shape=jax.ShapeDtypeStruct((8, 128), jnp.float...  63 us

profile of v2, /device:TPU:1, one launch (start us, length us, event | category | flops | bytes accessed | tf_op | source)
XLA Modules:
  0.0 64.3 jit_solution(10857533148424042506)
XLA Ops:
  0.0 0.0 copy-start
  0.0 63.0 %shard_map.46 = f32[8,128]{1,0:T(8,128)} custom-call(s32[3,24]{1,0:T(4,128)} %anc.1, bf16[512,1024]{1,0:T(8,128)(2,1)} %root.1, bf16[3,3,256,128]{3,2,1,0:T(8,128)(2,1)} %bitcast.1), custom_call_target="tpu_custom_call" | custom-call | tf_op jit(solution)/shard_map/pallas_call | solution.py:439
  63.0 0.0 copy-done
  63.0 1.3 %slice_add_fusion = f32[3,128]{1,0:T(4,128)} fusion(f32[3,128]{1,0:T(4,128)S(1)} %copy-done, f32[8,128]{1,0:T(8,128)} %shard_map.46), kind=kLoop, calls=%fused_computation | loop fusion | flops 384 | bytes 4608 | tf_op jit(solution)/shard_map/add | solution.py:474
Async XLA Ops:
  0.0 63.0 %copy-start = (f32[3,128]{1,0:T(4,128)S(1)}, f32[3,128]{1,0:T(4,128)}, u32[]{:S(2)}) copy-start(f32[3,128]{1,0:T(4,128)} %param.7) | copy-start | bytes 4612

commit v3 on v2

--- a/solution.py
+++ b/solution.py
@@ -10,11 +10,17 @@
 CHILDREN = 3
 ROOT_BLOCKS = 32
 MAX_ANC = 24
-Z_FIRST = (1, 2, 2)
-FAR_UP = (1, 1, 0)
+Z_FIRST = (3, 0, 2)
+FAR_UP = (0, 2, 0)
 SOURCES = ((0, 0), (0, 1), (1, 0), (3, 0), (1, 1), (3, 1), (2, 0), (2, 1))
 UNITS = 2 * len(SOURCES)
-COPIES = 96
+ORDER = (
+    ("a0", "bd0", "bu0", "ra1", "rb0u", "rb1d", "a1", "bd1", "bu1", "ra0", "rb0d", "rb1u", "a2", "cd0", "cu0"),
+    ("near", "rd0u", "rd1d", "re1u", "dd1", "du1", "ed1", "bd2", "bu2", "rc0d", "eu1", "rd1u", "re1d", "ks2"),
+    ("do0", "du0", "rc0u", "ka1", "opposite", "ef1", "cd2", "rd0d", "re1f", "du2", "dd2", "ed2", "cu2", "eu2"),
+    ("kb0", "ka0", "do2", "kb1", "ef2", "ka2", "ku2", "kd2", "kf2"),
+)
+COPIES = sum(len(line) for line in ORDER) - 2
 
 
 def pick(index, values):
@@ -37,13 +43,10 @@
     pk0,
     pk1,
     pk2,
-    acc,
     part,
     red,
     slot_of,
     listed,
-    unit_row,
-    unit_win,
     local_sem,
     send_sem,
     recv_sem,
@@ -111,12 +114,12 @@
     def _():
         local_ext.start()
 
-    group = [(dy, dc, dz) for dy in range(4) for dc in range(2) for dz in range(2)][1:]
+    group = [(dy, dc, dz) for dy in (2, 1, 3, 0) for dz in (1, 0) for dc in (1, 0)][:-1]
 
     def member(dy, dc, dz):
         return device(x, (y + dy) % 4, zp if dz else z, 1 - core if dc else core)
 
-    partners = [member(*g) for g in group] + [d_zq, d_xu, d_xd]
+    partners = [d_z, d_yu, d_yd, d_core, d_zq, d_xu, d_xd]
     barrier = pltpu.get_barrier_semaphore()
     for partner in partners:
         pl.semaphore_signal(barrier, inc=1, device_id=partner, device_id_type=MESH)
@@ -131,11 +134,79 @@
 
     pl.semaphore_wait(barrier, len(partners))
 
-    sent = []
-
-    def send(src, dst, target):
+    sent, arrived = {}, set()
+
+    def slots(c, zz, py, lo, hi):
+        return pb[c].at[zz, py, pl.ds(core * 3 + lo, hi - lo)]
+
+    def unit(dx, zr, t, lo=0, hi=BLK):
+        ref = rb.at[2 * SOURCES.index((dx, zr)) + t]
+        return ref if hi - lo == BLK else ref.at[pl.ds(lo, hi - lo)]
+
+    def rows_copy(kind, c):
+        m = Z_FIRST[c]
+        split = m + FAR_UP[c]
+        same = {
+            "bu": (slots(c, 0, y, 0, 3), d_yu, ()),
+            "bd": (slots(c, 0, y, 0, 3), d_yd, ()),
+            "cu": (slots(c, 1, y, 0, m), d_yu, ("a",)),
+            "cd": (slots(c, 1, y, 0, m), d_yd, ("a",)),
+            "du": (slots(c, 0, down, 0, split), d_yu, ("bu",)),
+            "dd": (slots(c, 0, up, split, 3), d_yd, ("bd",)),
+            "do": (slots(c, 1, up, 0, m), d_yd, ("cd",)),
+            "ka": (pb[c].at[0, :, pl.ds(core * 3, 3)], d_core, ("bu", "bd", "du", "dd")),
+            "kb": (pb[c].at[1, :, pl.ds(core * 3, 3)], d_core, ("a", "cu", "cd", "do", "eu", "ed", "ef")),
+            "ks": (slots(c, 1, y, 0, 3), d_core, ("a",)),
+            "kd": (slots(c, 1, down, 0, 3), d_core, ("cu", "ed")),
+            "ku": (slots(c, 1, up, 0, 3), d_core, ("cd", "eu")),
+            "kf": (slots(c, 1, far, 0, 3), d_core, ("do", "ef")),
+        }
+        over = {
+            "a": (y, 0, ()),
+            "ed": (down, m, ("bu",)),
+            "eu": (up, m, ("bd",)),
+            "ef": (far, m, ("du", "dd")),
+        }
+        if kind in same:
+            ref, target, first = same[kind]
+            return ref, ref, target, first
+        py, lo, first = over[kind]
+        return slots(c, 0, py, lo, 3), slots(c, 1, py, lo, 3), d_z, first
+
+    half = BLK // 2
+    root_copies = {
+        "ra0": (unit(0, 0, 0), unit(0, 1, 0), d_zq, ()),
+        "ra1": (unit(0, 0, 1), unit(0, 1, 1), d_zq, ()),
+        "rb0u": (unit(0, 0, 0), unit(3, 0, 0), d_xu, ()),
+        "rb0d": (unit(0, 0, 0), unit(1, 0, 0), d_xd, ()),
+        "rb1u": (unit(0, 0, 1), unit(3, 0, 1), d_xu, ()),
+        "rb1d": (unit(0, 0, 1), unit(1, 0, 1), d_xd, ()),
+        "rc0u": (unit(0, 1, 0), unit(3, 1, 0), d_xu, ("ra0",)),
+        "rc0d": (unit(0, 1, 0), unit(1, 1, 0), d_xd, ("ra0",)),
+        "rd0u": (unit(3, 0, 0), unit(2, 0, 0), d_xu, ("rb0u",)),
+        "rd0d": (unit(1, 1, 0), unit(2, 1, 0), d_xd, ("rc0d",)),
+        "rd1u": (unit(3, 0, 1, 0, half), unit(2, 0, 1, 0, half), d_xu, ("rb1u",)),
+        "rd1d": (unit(1, 0, 1, half, BLK), unit(2, 0, 1, half, BLK), d_xd, ("rb1d",)),
+        "re1d": (unit(3, 0, 1), unit(3, 1, 1), d_zq, ("rb1u",)),
+        "re1u": (unit(1, 0, 1), unit(1, 1, 1), d_zq, ("rb1d",)),
+        "re1f": (unit(2, 0, 1), unit(2, 1, 1), d_zq, ("rd1u", "rd1d")),
+    }
+
+    def arrive(names):
+        for name in names:
+            if name in sent and name not in arrived:
+                sent[name].wait_recv()
+                arrived.add(name)
+
+    def send(name):
+        if name in root_copies:
+            src, dst, target, first = root_copies[name]
+        else:
+            src, dst, target, first = rows_copy(name[:-1], int(name[-1]))
+            first = [kind + name[-1] for kind in first]
+        arrive(first)
         n = len(sent)
-        copy = pltpu.make_async_remote_copy(
+        sent[name] = pltpu.make_async_remote_copy(
             src_ref=src,
             dst_ref=dst,
             send_sem=send_sem.at[n],
@@ -143,51 +214,7 @@
             device_id=target,
             device_id_type=MESH,
         )
-        copy.start()
-        sent.append(copy)
-        return copy
-
-    def slots(c, zz, py, lo, hi):
-        return pb[c].at[zz, py, pl.ds(core * 3 + lo, hi - lo)]
-
-    def unit(dx, zr, t):
-        return rb.at[2 * SOURCES.index((dx, zr)) + t]
-
-    def p_a(c):
-        return send(slots(c, 0, y, 0, 3), slots(c, 1, y, 0, 3), d_z)
-
-    def p_b(c):
-        own = slots(c, 0, y, 0, 3)
-        return send(own, own, d_yu), send(own, own, d_yd)
-
-    def p_c(c):
-        ref = slots(c, 1, y, 0, Z_FIRST[c])
-        return send(ref, ref, d_yu), send(ref, ref, d_yd)
-
-    def p_d_up(c):
-        ref = slots(c, 0, down, 0, Z_FIRST[c] + FAR_UP[c])
-        return send(ref, ref, d_yu)
-
-    def p_d_down(c):
-        if Z_FIRST[c] + FAR_UP[c] == 3:
-            return None
-        ref = slots(c, 0, up, Z_FIRST[c] + FAR_UP[c], 3)
-        return send(ref, ref, d_yd)
-
-    def p_d_other(c):
-        ref = slots(c, 1, up, 0, Z_FIRST[c])
-        return send(ref, ref, d_yd)
-
-    def p_e(c, py):
-        return send(slots(c, 0, py, Z_FIRST[c], 3), slots(c, 1, py, Z_FIRST[c], 3), d_z)
-
-    def p_core(c, zz, py, lo, hi):
-        ref = slots(c, zz, py, lo, hi)
-        return send(ref, ref, d_core)
-
-    def p_core_all(c):
-        ref = pb[c].at[:, :, pl.ds(core * 3, 3)]
-        return send(ref, ref, d_core)
+        sent[name].start()
 
     ext_is_mine = z_ext == z
     dx_ext = (x - y + 4) % 4
@@ -231,16 +258,8 @@
         to_xd.start()
         to_zq.start()
 
-    a, b, cc, du, dd, do, e = {}, {}, {}, {}, {}, {}, {}
-    kids = []
-    a[0] = p_a(0)
-    b[0] = p_b(0)
-    r_a0 = send(unit(0, 0, 0), unit(0, 1, 0), d_zq)
-    r_b1 = send(unit(0, 0, 1), unit(3, 0, 1), d_xu), send(unit(0, 0, 1), unit(1, 0, 1), d_xd)
-    r_a1 = send(unit(0, 0, 1), unit(0, 1, 1), d_zq)
-    r_b0 = send(unit(0, 0, 0), unit(3, 0, 0), d_xu), send(unit(0, 0, 0), unit(1, 0, 0), d_xd)
-    a[1] = p_a(1)
-    b[1] = p_b(1)
+    for name in ORDER[0]:
+        send(name)
 
     for c in range(CHILDREN):
 
@@ -251,13 +270,11 @@
             return jnp.minimum(at + hit, MAX_ANC - 1)
 
         lax.fori_loop(0, ROOT_BLOCKS, find, jnp.int32(0))
-    for at, (dx, zr) in enumerate(SOURCES):
+    part[...] = jnp.zeros_like(part)
+    units = []
+    for dx, zr in SOURCES:
         px, pz = (x + dx) % 4, zq if zr else z
-        for t in range(2):
-            unit_row[2 * at + t] = 2 * (px * 4 + pz) + t
-            unit_win[2 * at + t] = window(px, pz, t)
-    acc[...] = jnp.zeros_like(acc)
-    part[...] = jnp.zeros_like(part)
+        units += [(2 * (px * 4 + pz) + t, window(px, pz, t)) for t in range(2)]
 
     def build(c):
         for at, key in enumerate((3, 0, 2, 1, 3)):
@@ -268,134 +285,50 @@
                     pb[c][zz, slot // 6, slot % 6] * keep
                 )
 
+    acc = [[jnp.zeros((8, 128), jnp.float32)] * 2 for _ in range(CHILDREN)]
+
     def add(c, product, row):
         slot, keep = slot_of[c, row], listed[c, row]
         for zz in range(2):
             mine = pb[c][zz, slot // 6, slot % 6].astype(jnp.float32)
             term = product[:, zz * 128 : (zz + 1) * 128] * mine
-            acc[c, zz] += jnp.sum(term.reshape(BLK // 8, 8, 128), axis=0) * keep
-
-    def compute(c, lo, hi):
-        def step(u, carry):
-            start = pl.multiple_of(unit_win[u] * BLK, BLK)
+            acc[c][zz] = acc[c][zz] + jnp.sum(term.reshape(BLK // 8, 8, 128), axis=0) * keep
+
+    def compute(c):
+        for u, (row, win) in enumerate(units):
+            start = pl.multiple_of(win * BLK, BLK)
             product = jnp.dot(
                 rb[u], pk[c][pl.ds(start, 2 * BLK), :], preferred_element_type=jnp.float32
             )
-            add(c, product, unit_row[u])
-            return carry
-
-        lax.fori_loop(lo, hi, step, 0)
-
-    def compute_ext(c):
+            add(c, product, row)
         start = pl.multiple_of(ext_key * BLK, BLK)
         product = jnp.dot(
             ext[...], pk[c][pl.ds(start, BLK), :], preferred_element_type=jnp.float32
         )
         add(c, product, ext_row)
 
-    def after_b(c):
-        b[c][0].wait_recv()
-        b[c][1].wait_recv()
-        du[c] = p_d_up(c)
-        dd[c] = p_d_down(c)
-        e[c] = [p_e(c, down), p_e(c, up)]
-
-    def after_a(c):
-        a[c].wait_recv()
-        cc[c] = p_c(c)
-
-    def after_c(c):
-        cc[c][0].wait_recv()
-        cc[c][1].wait_recv()
-        do[c] = p_d_other(c)
-
-    def after_d(c):
-        du[c].wait_recv()
-        if dd[c] is not None:
-            dd[c].wait_recv()
-        e[c].append(p_e(c, far))
-
-    after_a(0)
-    after_b(0)
-    r_a0.wait_recv()
-    r_c0 = send(unit(0, 1, 0), unit(3, 1, 0), d_xu), send(unit(0, 1, 0), unit(1, 1, 0), d_xd)
-    r_b1[0].wait_recv()
-    r_b1[1].wait_recv()
-    half = BLK // 2
-    r_d1 = (
-        send(unit(3, 0, 1).at[pl.ds(0, half)], unit(2, 0, 1).at[pl.ds(0, half)], d_xu),
-        send(unit(1, 0, 1).at[pl.ds(half, half)], unit(2, 0, 1).at[pl.ds(half, half)], d_xd),
-    )
-    r_e1 = [send(unit(3, 0, 1), unit(3, 1, 1), d_zq), send(unit(1, 0, 1), unit(1, 1, 1), d_zq)]
-    ext_on(near, True)
-    after_c(0)
-    a[2] = p_a(2)
-    b[2] = p_b(2)
-    after_a(1)
-    after_b(1)
-    after_d(0)
-    r_b0[0].wait_recv()
-    r_b0[1].wait_recv()
-    r_d0u = send(unit(3, 0, 0), unit(2, 0, 0), d_xu)
-    r_a1.wait_recv()
-    r_d1[0].wait_recv()
-    r_d1[1].wait_recv()
-    r_e1.append(send(unit(2, 0, 1), unit(2, 1, 1), d_zq))
-    after_c(1)
-    r_c0[0].wait_recv()
-    r_c0[1].wait_recv()
-    r_d0d = send(unit(1, 1, 0), unit(2, 1, 0), d_xd)
-    after_a(2)
-    after_b(2)
-    after_d(1)
-    do[0].wait_recv()
-    for copy in e[0]:
-        copy.wait_recv()
-    kids.append(p_core_all(0))
-    ext_on(opposite, False)
-    late = [p_core(2, 0, y, 0, 3), p_core(2, 0, up, 0, 3), p_core(2, 0, down, 0, 3), p_core(2, 1, y, 0, 3)]
-    after_c(2)
-    kids[0].wait_recv()
-    build(0)
-    compute(0, 0, 8)
-    after_d(2)
-    late.append(p_core(2, 0, far, 0, 3))
-    r_e1[0].wait_recv()
-    r_e1[1].wait_recv()
-    compute(0, 8, 12)
-    do[1].wait_recv()
-    for copy in e[1]:
-        copy.wait_recv()
-    kids.append(p_core_all(1))
-    r_d0u.wait_recv()
-    compute(0, 12, 14)
-    kids[1].wait_recv()
-    build(1)
-    compute(1, 0, 14)
-    r_d0d.wait_recv()
-    r_e1[2].wait_recv()
-    compute(0, 14, 16)
-    compute(1, 14, 16)
-    do[2].wait_recv()
-    for copy in e[2]:
-        copy.wait_recv()
-    for py in (down, up, far):
-        late.append(p_core(2, 1, py, 0, 3))
-    for copy in late:
-        copy.wait_recv()
-    build(2)
-    compute(2, 0, UNITS)
+    for name in ORDER[1] + ORDER[2] + ORDER[3]:
+        if name == "near":
+            ext_on(near, True)
+        elif name == "opposite":
+            ext_on(opposite, False)
+        else:
+            send(name)
+
+    arrive(root_copies)
 
     @pl.when(jnp.logical_not(ext_is_mine))
     def _():
         to_zq.wait_recv()
 
     for c in range(CHILDREN):
-        compute_ext(c)
+        arrive([name for name in sent if name not in root_copies and name[-1] == str(c)])
+        build(c)
+        compute(c)
 
     for zz in range(2):
         for c in range(CHILDREN):
-            part[zz, c : c + 1, :] = 2.0 * jnp.sum(acc[c, zz], axis=0, keepdims=True)
+            part[zz, c : c + 1, :] = 2.0 * jnp.sum(acc[c][zz], axis=0, keepdims=True)
     mine = q * 2 + z % 2
     sums = []
     for n, g in enumerate(group):
@@ -410,7 +343,7 @@
         copy.start()
         sums.append(copy)
     red[mine] = part[0]
-    for copy in sent:
+    for copy in sent.values():
         copy.wait_send()
 
     @pl.when(goes_zq)
@@ -452,13 +385,10 @@
         ]
         + [vmem((5 * BLK, 2 * 128), jnp.bfloat16)] * CHILDREN
         + [
-            vmem((CHILDREN, 2, 8, 128), jnp.float32),
             vmem((2, 8, 128), jnp.float32),
             vmem((16, 8, 128), jnp.float32),
             smem((CHILDREN, ROOT_BLOCKS), jnp.int32),
             smem((CHILDREN, ROOT_BLOCKS), jnp.float32),
-            smem((UNITS,), jnp.int32),
-            smem((UNITS,), jnp.int32),
             dma((8,)),
             dma((COPIES,)),
             dma((COPIES,)),

time: 64.5 us -> 52.5 us (0.81)
  Pallas kernels: 63 us -> 51.1 us
    pallas_call x1, Pallas kernels: 63 us -> 51.1 us  [per_device(): pl.pallas_call(kernel, out_shape=jax.ShapeDtypeStruct((8, 128), jnp.float...]
where the time goes in v3:
time: 52.5 us; the launch traced here: 52.3 us
  Pallas kernels  51.1 us (97%)
  other arithmetic  1.25 us (2%)
    pallas_call x1, Pallas kernels, per_device(): pl.pallas_call(kernel, out_shape=jax.ShapeDtypeStruct((8, 128), jnp.float...  51.1 us
    add x1, other arithmetic, per_device(): return diag_inverse + total[:CHILDREN]  1.25 us

profile of v3, /device:TPU:1, one launch (start us, length us, event | category | flops | bytes accessed | tf_op | source)
XLA Modules:
  0.0 52.3 jit_solution(8514928672925903626)
XLA Ops:
  0.0 0.0 copy-start
  0.0 51.1 %shard_map.46 = f32[8,128]{1,0:T(8,128)} custom-call(s32[3,24]{1,0:T(4,128)} %anc.1, bf16[512,1024]{1,0:T(8,128)(2,1)} %root.1, bf16[3,3,256,128]{3,2,1,0:T(8,128)(2,1)} %bitcast.1), custom_call_target="tpu_custom_call" | custom-call | tf_op jit(solution)/shard_map/pallas_call | solution.py:372
  51.1 0.0 copy-done
  51.1 1.3 %slice_add_fusion = f32[3,128]{1,0:T(4,128)} fusion(f32[3,128]{1,0:T(4,128)S(1)} %copy-done, f32[8,128]{1,0:T(8,128)} %shard_map.46), kind=kLoop, calls=%fused_computation | loop fusion | flops 384 | bytes 4608 | tf_op jit(solution)/shard_map/add | solution.py:404
Async XLA Ops:
  0.0 51.1 %copy-start = (f32[3,128]{1,0:T(4,128)S(1)}, f32[3,128]{1,0:T(4,128)}, u32[]{:S(2)}) copy-start(f32[3,128]{1,0:T(4,128)} %param.7) | copy-start | bytes 4612

commit v4 on v3

--- a/solution.py
+++ b/solution.py
@@ -15,12 +15,14 @@
 SOURCES = ((0, 0), (0, 1), (1, 0), (3, 0), (1, 1), (3, 1), (2, 0), (2, 1))
 UNITS = 2 * len(SOURCES)
 ORDER = (
-    ("a0", "bd0", "bu0", "ra1", "rb0u", "rb1d", "a1", "bd1", "bu1", "ra0", "rb0d", "rb1u", "a2", "cd0", "cu0"),
-    ("near", "rd0u", "rd1d", "re1u", "dd1", "du1", "ed1", "bd2", "bu2", "rc0d", "eu1", "rd1u", "re1d", "ks2"),
-    ("do0", "du0", "rc0u", "ka1", "opposite", "ef1", "cd2", "rd0d", "re1f", "du2", "dd2", "ed2", "cu2", "eu2"),
-    ("kb0", "ka0", "do2", "kb1", "ef2", "ka2", "ku2", "kd2", "kf2"),
+    ("a0", "bd0", "bu0", "ra1", "rb0u", "rb1d", "a1", "bd1", "bu1", "ra0", "rb0d", "rb1u", "a2", "cd0"),
+    ("cu0", "near", "rd0u", "rd1d", "re1u", "dd1", "du1", "ed1", "bd2", "bu2", "rc0d", "eu1", "rd1u", "re1d"),
+    ("ks2", "do0", "du0", "rc0u", "ka1", "opposite", "ef1", "cd2", "rd0d", "re1f", "du2", "dd2", "ed2", "cu2"),
+    ("eu2", "kb0", "ka0", "do2", "kb1", "ef2", "ka2", "sum0", "sum1", "ku2", "kd2", "kf2"),
 )
-COPIES = sum(len(line) for line in ORDER) - 2
+ORDER = sum(ORDER, ())
+OTHER = ("near", "opposite", "sum0", "sum1")
+COPIES = len(ORDER) - len(OTHER)
 
 
 def pick(index, values):
@@ -31,7 +33,7 @@
 
 
 def kernel(
-    anc,
+    anc_hbm,
     root,
     rows,
     out,
@@ -45,6 +47,7 @@
     pk2,
     part,
     red,
+    anc,
     slot_of,
     listed,
     local_sem,
@@ -72,6 +75,15 @@
     d_xu, d_xd = device((x + 1) % 4, y, z, core), device((x + 3) % 4, y, z, core)
     d_core = device(x, y, z, 1 - core)
 
+    group = [(dy, dc, dz) for dy in (2, 1, 3, 0) for dz in (1, 0) for dc in (1, 0)][:-1]
+
+    def member(dy, dc, dz):
+        return device(x, (y + dy) % 4, zp if dz else z, 1 - core if dc else core)
+
+    partners = [d_z, d_yu, d_yd, d_core, d_zq, d_xu, d_xd]
+    barrier = pltpu.get_barrier_semaphore()
+    for partner in partners:
+        pl.semaphore_signal(barrier, inc=1, device_id=partner, device_id_type=MESH)
     def window(px, pz, t):
         diagonal = jnp.logical_and(px == y, pz // 2 == core)
         second = pz - 2 * core
@@ -109,20 +121,13 @@
     )
     for copy in local:
         copy.start()
+    blocks = pltpu.make_async_copy(anc_hbm, anc, local_sem.at[8])
+    blocks.start()
 
     @pl.when(own_diag)
     def _():
         local_ext.start()
 
-    group = [(dy, dc, dz) for dy in (2, 1, 3, 0) for dz in (1, 0) for dc in (1, 0)][:-1]
-
-    def member(dy, dc, dz):
-        return device(x, (y + dy) % 4, zp if dz else z, 1 - core if dc else core)
-
-    partners = [d_z, d_yu, d_yd, d_core, d_zq, d_xu, d_xd]
-    barrier = pltpu.get_barrier_semaphore()
-    for partner in partners:
-        pl.semaphore_signal(barrier, inc=1, device_id=partner, device_id_type=MESH)
     for copy in local:
         copy.wait()
 
@@ -258,9 +263,11 @@
         to_xd.start()
         to_zq.start()
 
-    for name in ORDER[0]:
+    free = next(n for n, name in enumerate(ORDER) if name[0] in "cdek")
+    for name in ORDER[:free]:
         send(name)
 
+    blocks.wait()
     for c in range(CHILDREN):
 
         def find(block, at, c=c):
@@ -294,72 +301,104 @@
             term = product[:, zz * 128 : (zz + 1) * 128] * mine
             acc[c][zz] = acc[c][zz] + jnp.sum(term.reshape(BLK // 8, 8, 128), axis=0) * keep
 
-    def compute(c):
-        for u, (row, win) in enumerate(units):
+    brought = (
+        ((), ()),
+        (("ra0",), ("ra1",)),
+        (("rb0d",), ("rb1d",)),
+        (("rb0u",), ("rb1u",)),
+        (("rc0d",), ("re1u",)),
+        (("rc0u",), ("re1d",)),
+        (("rd0u",), ("rd1u", "rd1d")),
+        (("rd0d",), ("re1f",)),
+    )
+    late = UNITS - 2
+
+    def compute(c, lo, hi):
+        for u in range(lo, hi):
+            arrive(brought[u // 2][u % 2])
+            row, win = units[u]
             start = pl.multiple_of(win * BLK, BLK)
             product = jnp.dot(
                 rb[u], pk[c][pl.ds(start, 2 * BLK), :], preferred_element_type=jnp.float32
             )
             add(c, product, row)
+
+    def compute_ext(c):
         start = pl.multiple_of(ext_key * BLK, BLK)
         product = jnp.dot(
             ext[...], pk[c][pl.ds(start, BLK), :], preferred_element_type=jnp.float32
         )
         add(c, product, ext_row)
 
-    for name in ORDER[1] + ORDER[2] + ORDER[3]:
+    def complete(c):
+        arrive([name for name in sent if name[0] != "r" and name[-1] == str(c)])
+        build(c)
+
+    for name in ORDER[free:]:
         if name == "near":
             ext_on(near, True)
         elif name == "opposite":
             ext_on(opposite, False)
+        elif name[:3] == "sum":
+            complete(int(name[3]))
+            compute(int(name[3]), 0, late)
         else:
             send(name)
 
-    arrive(root_copies)
-
     @pl.when(jnp.logical_not(ext_is_mine))
     def _():
         to_zq.wait_recv()
 
-    for c in range(CHILDREN):
-        arrive([name for name in sent if name not in root_copies and name[-1] == str(c)])
-        build(c)
-        compute(c)
+    for c in range(2):
+        compute(c, late, UNITS)
+        compute_ext(c)
+    gone = [name for name in sent if name[0] != "k"]
+    for name in gone:
+        sent[name].wait_send()
+
+    @pl.when(goes_zq)
+    def _():
+        to_zq.wait_send()
+
+    @pl.when(goes_xu)
+    def _():
+        to_xu.wait_send()
+
+    @pl.when(goes_xd)
+    def _():
+        to_xd.wait_send()
+
+    complete(2)
+    compute(2, 0, UNITS)
+    compute_ext(2)
 
     for zz in range(2):
         for c in range(CHILDREN):
             part[zz, c : c + 1, :] = 2.0 * jnp.sum(acc[c][zz], axis=0, keepdims=True)
     mine = q * 2 + z % 2
-    sums = []
-    for n, g in enumerate(group):
-        copy = pltpu.make_async_remote_copy(
+    for g in group:
+        pltpu.make_async_remote_copy(
             src_ref=part.at[g[2]],
             dst_ref=red.at[mine],
-            send_sem=red_send.at[n],
-            recv_sem=red_recv.at[n],
+            send_sem=red_send,
+            recv_sem=red_recv,
             device_id=member(*g),
             device_id_type=MESH,
-        )
-        copy.start()
-        sums.append(copy)
+        ).start()
     red[mine] = part[0]
-    for copy in sent.values():
-        copy.wait_send()
-
-    @pl.when(goes_zq)
-    def _():
-        to_zq.wait_send()
-
-    @pl.when(goes_xu)
-    def _():
-        to_xu.wait_send()
-
-    @pl.when(goes_xd)
-    def _():
-        to_xd.wait_send()
-
-    for copy in sums:
-        copy.wait()
+    for name in sent:
+        if name not in gone:
+            sent[name].wait_send()
+    every = pltpu.make_async_remote_copy(
+        src_ref=red.at[pl.ds(0, 15)],
+        dst_ref=red.at[pl.ds(0, 15)],
+        send_sem=red_send,
+        recv_sem=red_recv,
+        device_id=d_core,
+        device_id_type=MESH,
+    )
+    every.wait_recv()
+    every.wait_send()
     total = red[0]
     for at in range(1, 16):
         total = total + red[at]
@@ -371,9 +410,9 @@
     rows = factor_rows.reshape(CHILDREN, 3, BLK, 128)
     total = pl.pallas_call(
         kernel,
-        out_shape=jax.ShapeDtypeStruct((8, 128), jnp.float32),
+        out_shape=vmem((8, 128), jnp.float32),
         in_specs=[
-            pl.BlockSpec(memory_space=smem),
+            pl.BlockSpec(memory_space=pl.ANY),
             pl.BlockSpec(memory_space=pl.ANY),
             pl.BlockSpec(memory_space=pl.ANY),
         ],
@@ -387,15 +426,16 @@
         + [
             vmem((2, 8, 128), jnp.float32),
             vmem((16, 8, 128), jnp.float32),
+            smem((CHILDREN, MAX_ANC), jnp.int32),
             smem((CHILDREN, ROOT_BLOCKS), jnp.int32),
             smem((CHILDREN, ROOT_BLOCKS), jnp.float32),
-            dma((8,)),
+            dma((9,)),
             dma((COPIES,)),
             dma((COPIES,)),
             dma((3,)),
             dma,
-            dma((15,)),
-            dma((15,)),
+            dma,
+            dma,
         ],
         compiler_params=pltpu.CompilerParams(
             collective_id=0, has_side_effects=True, vmem_limit_bytes=62 * 2**20

time: 52.5 us -> 49 us (0.933)
  Pallas kernels: 51.1 us -> 48.3 us
  other arithmetic: 1.25 us -> 0.58 us
    pallas_call x1, Pallas kernels: 51.1 us -> 48.3 us  [per_device(): pl.pallas_call(kernel, out_shape=vmem((8, 128), jnp.float32), in_specs=[p...]
    add x1, other arithmetic: 1.25 us -> 0.58 us  [per_device(): return diag_inverse + total[:CHILDREN]]
where the time goes in v4:
time: 49 us; the launch traced here: 48.9 us
  Pallas kernels  48.3 us (99%)
  other arithmetic  0.58 us (1%)
    pallas_call x1, Pallas kernels, per_device(): pl.pallas_call(kernel, out_shape=vmem((8, 128), jnp.float32), in_specs=[p...  48.3 us

profile of v4, /device:TPU:1, one launch (start us, length us, event | category | flops | bytes accessed | tf_op | source)
XLA Modules:
  0.0 48.9 jit_solution(3854660751915318363)
XLA Ops:
  0.0 0.0 copy-start
  0.0 48.3 %shard_map.46 = f32[8,128]{1,0:T(8,128)S(1)} custom-call(s32[3,24]{1,0:T(4,128)} %anc_hbm.1, bf16[512,1024]{1,0:T(8,128)(2,1)} %root.1, bf16[3,3,256,128]{3,2,1,0:T(8,128)(2,1)} %bitcast.1), custom_call_target="tpu_custom_call" | custom-call | tf_op jit(solution)/shard_map/pallas_call | solution.py:411
  48.3 0.0 copy-done
  48.3 0.6 %slice_add_fusion = f32[3,128]{1,0:T(4,128)} fusion(f32[3,128]{1,0:T(4,128)S(1)} %copy-done, f32[8,128]{1,0:T(8,128)S(1)} %shard_map.46), kind=kLoop, calls=%fused_computation | loop fusion | flops 384 | bytes 4608 | tf_op jit(solution)/shard_map/add | solution.py:444
Async XLA Ops:
  0.0 48.3 %copy-start = (f32[3,128]{1,0:T(4,128)S(1)}, f32[3,128]{1,0:T(4,128)}, u32[]{:S(2)}) copy-start(f32[3,128]{1,0:T(4,128)} %param.7) | copy-start | bytes 4612

commit v5 on v4

--- a/solution.py
+++ b/solution.py
@@ -15,14 +15,14 @@
 SOURCES = ((0, 0), (0, 1), (1, 0), (3, 0), (1, 1), (3, 1), (2, 0), (2, 1))
 UNITS = 2 * len(SOURCES)
 ORDER = (
-    ("a0", "bd0", "bu0", "ra1", "rb0u", "rb1d", "a1", "bd1", "bu1", "ra0", "rb0d", "rb1u", "a2", "cd0"),
-    ("cu0", "near", "rd0u", "rd1d", "re1u", "dd1", "du1", "ed1", "bd2", "bu2", "rc0d", "eu1", "rd1u", "re1d"),
-    ("ks2", "do0", "du0", "rc0u", "ka1", "opposite", "ef1", "cd2", "rd0d", "re1f", "du2", "dd2", "ed2", "cu2"),
-    ("eu2", "kb0", "ka0", "do2", "kb1", "ef2", "ka2", "sum0", "sum1", "ku2", "kd2", "kf2"),
+    ("bd0", "bu1", "rb1d", "a0", "bd1", "ra0", "rb1u", "a1", "bu0", "bu2", "ra1", "cd0", "ed1"),
+    ("rb0u", "a2", "rb0d", "rc0d", "rd1d", "re1u", "du1", "re1d", "near", "dd1", "bd2", "rd1u", "do0"),
+    ("du0", "rc0u", "eu1", "cu0", "du2", "ef1", "cd2", "opposite", "rd0d", "rd0u", "eu2", "ka0", "ka1"),
+    ("ed2", "re1f", "cu2", "dd2", "kb0", "do2", "kb1", "ef2", "m0:0:8", "ka2", "m1:12:14", "ku2", "m0:12:14"),
+    ("m1:8:12", "kd2", "ks2", "m0:14:16", "kf2", "m0:8:12", "m1:0:8", "m1:14:16", "m2:8:14", "m2:0:8", "m2:14:16"),
 )
 ORDER = sum(ORDER, ())
-OTHER = ("near", "opposite", "sum0", "sum1")
-COPIES = len(ORDER) - len(OTHER)
+COPIES = sum(name[0] in "abcdekr" for name in ORDER)
 
 
 def pick(index, values):
@@ -263,7 +263,7 @@
         to_xd.start()
         to_zq.start()
 
-    free = next(n for n, name in enumerate(ORDER) if name[0] in "cdek")
+    free = next(n for n, name in enumerate(ORDER) if name[0] in "cdekmno")
     for name in ORDER[:free]:
         send(name)
 
@@ -311,7 +311,6 @@
         (("rd0u",), ("rd1u", "rd1d")),
         (("rd0d",), ("re1f",)),
     )
-    late = UNITS - 2
 
     def compute(c, lo, hi):
         for u in range(lo, hi):
@@ -330,47 +329,32 @@
         )
         add(c, product, ext_row)
 
-    def complete(c):
-        arrive([name for name in sent if name[0] != "r" and name[-1] == str(c)])
-        build(c)
-
+    def extra():
+        @pl.when(jnp.logical_not(ext_is_mine))
+        def _():
+            to_zq.wait_recv()
+
+        for c in range(CHILDREN - 1):
+            compute_ext(c)
+
+    complete = set()
     for name in ORDER[free:]:
         if name == "near":
             ext_on(near, True)
         elif name == "opposite":
             ext_on(opposite, False)
-        elif name[:3] == "sum":
-            complete(int(name[3]))
-            compute(int(name[3]), 0, late)
+        elif name[0] == "m":
+            c, lo, hi = (int(number) for number in name[1:].split(":"))
+            if c not in complete:
+                if c == CHILDREN - 1:
+                    extra()
+                arrive([copy for copy in sent if copy[0] != "r" and copy[-1] == str(c)])
+                build(c)
+                complete.add(c)
+            compute(c, lo, hi)
         else:
             send(name)
-
-    @pl.when(jnp.logical_not(ext_is_mine))
-    def _():
-        to_zq.wait_recv()
-
-    for c in range(2):
-        compute(c, late, UNITS)
-        compute_ext(c)
-    gone = [name for name in sent if name[0] != "k"]
-    for name in gone:
-        sent[name].wait_send()
-
-    @pl.when(goes_zq)
-    def _():
-        to_zq.wait_send()
-
-    @pl.when(goes_xu)
-    def _():
-        to_xu.wait_send()
-
-    @pl.when(goes_xd)
-    def _():
-        to_xd.wait_send()
-
-    complete(2)
-    compute(2, 0, UNITS)
-    compute_ext(2)
+    compute_ext(CHILDREN - 1)
 
     for zz in range(2):
         for c in range(CHILDREN):
@@ -386,9 +370,21 @@
             device_id_type=MESH,
         ).start()
     red[mine] = part[0]
-    for name in sent:
-        if name not in gone:
-            sent[name].wait_send()
+    for copy in sent.values():
+        copy.wait_send()
+
+    @pl.when(goes_zq)
+    def _():
+        to_zq.wait_send()
+
+    @pl.when(goes_xu)
+    def _():
+        to_xu.wait_send()
+
+    @pl.when(goes_xd)
+    def _():
+        to_xd.wait_send()
+
     every = pltpu.make_async_remote_copy(
         src_ref=red.at[pl.ds(0, 15)],
         dst_ref=red.at[pl.ds(0, 15)],

time: 49 us -> 47.8 us (0.976)
  Pallas kernels: 48.3 us -> 47.1 us
    pallas_call x1, Pallas kernels: 48.3 us -> 47.1 us  [per_device(): pl.pallas_call(kernel, out_shape=vmem((8, 128), jnp.float32), in_specs=[p...]
where the time goes in v5:
time: 47.8 us; the launch traced here: 47.7 us
  Pallas kernels  47.1 us (99%)
  other arithmetic  0.58 us (1%)
    pallas_call x1, Pallas kernels, per_device(): pl.pallas_call(kernel, out_shape=vmem((8, 128), jnp.float32), in_specs=[p...  47.1 us

profile of v5, /device:TPU:1, one launch (start us, length us, event | category | flops | bytes accessed | tf_op | source)
XLA Modules:
  0.0 47.7 jit_solution(15042653482546552754)
XLA Ops:
  0.0 0.0 copy-start
  0.0 47.1 %shard_map.46 = f32[8,128]{1,0:T(8,128)S(1)} custom-call(s32[3,24]{1,0:T(4,128)} %anc_hbm.1, bf16[512,1024]{1,0:T(8,128)(2,1)} %root.1, bf16[3,3,256,128]{3,2,1,0:T(8,128)(2,1)} %bitcast.1), custom_call_target="tpu_custom_call" | custom-call | tf_op jit(solution)/shard_map/pallas_call | solution.py:407
  47.1 0.0 copy-done
  47.1 0.6 %slice_add_fusion = f32[3,128]{1,0:T(4,128)} fusion(f32[3,128]{1,0:T(4,128)S(1)} %copy-done, f32[8,128]{1,0:T(8,128)S(1)} %shard_map.46), kind=kLoop, calls=%fused_computation | loop fusion | flops 384 | bytes 4608 | tf_op jit(solution)/shard_map/add | solution.py:440
Async XLA Ops:
  0.0 47.1 %copy-start = (f32[3,128]{1,0:T(4,128)S(1)}, f32[3,128]{1,0:T(4,128)}, u32[]{:S(2)}) copy-start(f32[3,128]{1,0:T(4,128)} %param.7) | copy-start | bytes 4612

commit v6 on v5

--- a/solution.py
+++ b/solution.py
@@ -15,11 +15,11 @@
 SOURCES = ((0, 0), (0, 1), (1, 0), (3, 0), (1, 1), (3, 1), (2, 0), (2, 1))
 UNITS = 2 * len(SOURCES)
 ORDER = (
-    ("bd0", "bu1", "rb1d", "a0", "bd1", "ra0", "rb1u", "a1", "bu0", "bu2", "ra1", "cd0", "ed1"),
-    ("rb0u", "a2", "rb0d", "rc0d", "rd1d", "re1u", "du1", "re1d", "near", "dd1", "bd2", "rd1u", "do0"),
-    ("du0", "rc0u", "eu1", "cu0", "du2", "ef1", "cd2", "opposite", "rd0d", "rd0u", "eu2", "ka0", "ka1"),
-    ("ed2", "re1f", "cu2", "dd2", "kb0", "do2", "kb1", "ef2", "m0:0:8", "ka2", "m1:12:14", "ku2", "m0:12:14"),
-    ("m1:8:12", "kd2", "ks2", "m0:14:16", "kf2", "m0:8:12", "m1:0:8", "m1:14:16", "m2:8:14", "m2:0:8", "m2:14:16"),
+    ("bd1", "bu1", "rb1u", "rb0u", "a0", "bd0", "a2", "rb0d", "bu0", "ra0", "ra1", "eu1", "cd0"),
+    ("rb1d", "a1", "du1", "bu2", "bd2", "ed1", "near", "rc0u", "rc0d", "dd1", "du0", "re1d", "rd1u"),
+    ("cu0", "do0", "rd1d", "cd2", "re1u", "opposite", "ef1", "ks2", "rd0d", "rd0u", "ka0", "du2", "re1f"),
+    ("ka1", "dd2", "eu2", "cu2", "ed2", "kb0", "do2", "kb1", "ef2", "ka2", "m0:8:12", "ku2", "m0:12:14"),
+    ("m0:0:8", "m1:12:14", "m1:8:12", "kd2", "kf2", "m1:14:16", "m1:0:8", "m0:14:16", "m2:8:14", "m2:0:8", "m2:14:16"),
 )
 ORDER = sum(ORDER, ())
 COPIES = sum(name[0] in "abcdekr" for name in ORDER)
@@ -57,6 +57,7 @@
     ext_recv,
     red_send,
     red_recv,
+    ready,
 ):
     pb, pk = (pb0, pb1, pb2), (pk0, pk1, pk2)
     p, q = lax.axis_index("prow"), lax.axis_index("pcol")
@@ -80,10 +81,16 @@
     def member(dy, dc, dz):
         return device(x, (y + dy) % 4, zp if dz else z, 1 - core if dc else core)
 
-    partners = [d_z, d_yu, d_yd, d_core, d_zq, d_xu, d_xd]
+    partners = [d_z, d_yu, d_yd, d_core, d_xu, d_xd]
+    tells = z >= 2
     barrier = pltpu.get_barrier_semaphore()
     for partner in partners:
         pl.semaphore_signal(barrier, inc=1, device_id=partner, device_id_type=MESH)
+
+    @pl.when(jnp.logical_not(tells))
+    def _():
+        pl.semaphore_signal(barrier, inc=1, device_id=d_zq, device_id_type=MESH)
+
     def window(px, pz, t):
         diagonal = jnp.logical_and(px == y, pz // 2 == core)
         second = pz - 2 * core
@@ -137,7 +144,11 @@
         for t in range(2):
             rb[t, :, 0:BLK] = rb[t, :, 0:BLK] * jnp.bfloat16(0.5)
 
-    pl.semaphore_wait(barrier, len(partners))
+    pl.semaphore_wait(barrier, len(partners) + tells.astype(jnp.int32))
+
+    @pl.when(tells)
+    def _():
+        pl.semaphore_signal(ready, inc=1, device_id=d_zq, device_id_type=MESH)
 
     sent, arrived = {}, set()
 
@@ -210,6 +221,8 @@
             src, dst, target, first = rows_copy(name[:-1], int(name[-1]))
             first = [kind + name[-1] for kind in first]
         arrive(first)
+        if target is d_zq and not any(name[:2] == "ra" for name in sent):
+            open_zq()
         n = len(sent)
         sent[name] = pltpu.make_async_remote_copy(
             src_ref=src,
@@ -261,7 +274,15 @@
     def _():
         to_xu.start()
         to_xd.start()
-        to_zq.start()
+
+    def open_zq():
+        @pl.when(jnp.logical_not(tells))
+        def _():
+            pl.semaphore_wait(ready, 1)
+
+        @pl.when(own_diag)
+        def _():
+            to_zq.start()
 
     free = next(n for n, name in enumerate(ORDER) if name[0] in "cdekmno")
     for name in ORDER[:free]:
@@ -432,6 +453,7 @@
             dma,
             dma,
             dma,
+            pltpu.SemaphoreType.REGULAR,
         ],
         compiler_params=pltpu.CompilerParams(
             collective_id=0, has_side_effects=True, vmem_limit_bytes=62 * 2**20

time: 47.8 us -> 47.3 us (0.990)
  Pallas kernels: 47.1 us -> 46.6 us
    pallas_call x1, Pallas kernels: 47.1 us -> 46.6 us  [per_device(): pl.pallas_call(kernel, out_shape=vmem((8, 128), jnp.float32), in_specs=[p...]
where the time goes in v6:
time: 47.3 us; the launch traced here: 47.2 us
  Pallas kernels  46.6 us (99%)
  other arithmetic  0.58 us (1%)
    pallas_call x1, Pallas kernels, per_device(): pl.pallas_call(kernel, out_shape=vmem((8, 128), jnp.float32), in_specs=[p...  46.6 us

profile of v6, /device:TPU:1, one launch (start us, length us, event | category | flops | bytes accessed | tf_op | source)
XLA Modules:
  0.0 47.2 jit_solution(15946752764063852592)
XLA Ops:
  0.0 0.0 copy-start
  0.0 46.6 %shard_map.46 = f32[8,128]{1,0:T(8,128)S(1)} custom-call(s32[3,24]{1,0:T(4,128)} %anc_hbm.1, bf16[512,1024]{1,0:T(8,128)(2,1)} %root.1, bf16[3,3,256,128]{3,2,1,0:T(8,128)(2,1)} %bitcast.1), custom_call_target="tpu_custom_call" | custom-call | tf_op jit(solution)/shard_map/pallas_call | solution.py:428
  46.6 0.0 copy-done
  46.6 0.6 %slice_add_fusion = f32[3,128]{1,0:T(4,128)} fusion(f32[3,128]{1,0:T(4,128)S(1)} %copy-done, f32[8,128]{1,0:T(8,128)S(1)} %shard_map.46), kind=kLoop, calls=%fused_computation | loop fusion | flops 384 | bytes 4608 | tf_op jit(solution)/shard_map/add | solution.py:462
Async XLA Ops:
  0.0 46.6 %copy-start = (f32[3,128]{1,0:T(4,128)S(1)}, f32[3,128]{1,0:T(4,128)}, u32[]{:S(2)}) copy-start(f32[3,128]{1,0:T(4,128)} %param.7) | copy-start | bytes 4612

commit v7 on v6

--- a/solution.py
+++ b/solution.py
@@ -37,9 +37,12 @@
     root,
     rows,
     out,
-    pb0,
-    pb1,
-    pb2,
+    pb00,
+    pb01,
+    pb10,
+    pb11,
+    pb20,
+    pb21,
     rb,
     ext,
     pk0,
@@ -59,7 +62,7 @@
     red_recv,
     ready,
 ):
-    pb, pk = (pb0, pb1, pb2), (pk0, pk1, pk2)
+    pb, pk = ((pb00, pb01), (pb10, pb11), (pb20, pb21)), (pk0, pk1, pk2)
     p, q = lax.axis_index("prow"), lax.axis_index("pcol")
     x, z = p // 4, p % 4
     y, core = q // 2, q % 2
@@ -108,7 +111,7 @@
     for c in range(CHILDREN):
         local.append(
             pltpu.make_async_copy(
-                rows.at[c], pb[c].at[0, y, pl.ds(core * 3, 3)], local_sem.at[c]
+                rows.at[c], pb[c][0].at[y, pl.ds(core * 3, 3)], local_sem.at[c]
             )
         )
     for t in range(2):
@@ -153,7 +156,7 @@
     sent, arrived = {}, set()
 
     def slots(c, zz, py, lo, hi):
-        return pb[c].at[zz, py, pl.ds(core * 3 + lo, hi - lo)]
+        return pb[c][zz].at[py, pl.ds(core * 3 + lo, hi - lo)]
 
     def unit(dx, zr, t, lo=0, hi=BLK):
         ref = rb.at[2 * SOURCES.index((dx, zr)) + t]
@@ -170,8 +173,8 @@
             "du": (slots(c, 0, down, 0, split), d_yu, ("bu",)),
             "dd": (slots(c, 0, up, split, 3), d_yd, ("bd",)),
             "do": (slots(c, 1, up, 0, m), d_yd, ("cd",)),
-            "ka": (pb[c].at[0, :, pl.ds(core * 3, 3)], d_core, ("bu", "bd", "du", "dd")),
-            "kb": (pb[c].at[1, :, pl.ds(core * 3, 3)], d_core, ("a", "cu", "cd", "do", "eu", "ed", "ef")),
+            "ka": (pb[c][0].at[:, pl.ds(core * 3, 3)], d_core, ("bu", "bd", "du", "dd")),
+            "kb": (pb[c][1].at[:, pl.ds(core * 3, 3)], d_core, ("a", "cu", "cd", "do", "eu", "ed", "ef")),
             "ks": (slots(c, 1, y, 0, 3), d_core, ("a",)),
             "kd": (slots(c, 1, down, 0, 3), d_core, ("cu", "ed")),
             "ku": (slots(c, 1, up, 0, 3), d_core, ("cd", "eu")),
@@ -304,13 +307,13 @@
         px, pz = (x + dx) % 4, zq if zr else z
         units += [(2 * (px * 4 + pz) + t, window(px, pz, t)) for t in range(2)]
 
-    def build(c):
+    def build(c, halves=(0, 1)):
         for at, key in enumerate((3, 0, 2, 1, 3)):
             block = 4 * q + key
             slot, keep = slot_of[c, block], listed[c, block].astype(jnp.bfloat16)
-            for zz in range(2):
+            for zz in halves:
                 pk[c][at * BLK : (at + 1) * BLK, zz * 128 : (zz + 1) * 128] = (
-                    pb[c][zz, slot // 6, slot % 6] * keep
+                    pb[c][zz][slot // 6, slot % 6] * keep
                 )
 
     acc = [[jnp.zeros((8, 128), jnp.float32)] * 2 for _ in range(CHILDREN)]
@@ -318,7 +321,7 @@
     def add(c, product, row):
         slot, keep = slot_of[c, row], listed[c, row]
         for zz in range(2):
-            mine = pb[c][zz, slot // 6, slot % 6].astype(jnp.float32)
+            mine = pb[c][zz][slot // 6, slot % 6].astype(jnp.float32)
             term = product[:, zz * 128 : (zz + 1) * 128] * mine
             acc[c][zz] = acc[c][zz] + jnp.sum(term.reshape(BLK // 8, 8, 128), axis=0) * keep
 
@@ -367,10 +370,13 @@
         elif name[0] == "m":
             c, lo, hi = (int(number) for number in name[1:].split(":"))
             if c not in complete:
+                mine = [copy for copy in sent if copy[0] != "r" and copy[-1] == str(c)]
                 if c == CHILDREN - 1:
+                    arrive([copy for copy in mine if copy[:2] in ("bu", "bd", "du", "dd", "ka")])
+                    build(c, (0,))
                     extra()
-                arrive([copy for copy in sent if copy[0] != "r" and copy[-1] == str(c)])
-                build(c)
+                arrive(mine)
+                build(c, (1,) if c == CHILDREN - 1 else (0, 1))
                 complete.add(c)
             compute(c, lo, hi)
         else:
@@ -434,7 +440,7 @@
             pl.BlockSpec(memory_space=pl.ANY),
         ],
         out_specs=pl.BlockSpec(memory_space=vmem),
-        scratch_shapes=[vmem((2, 4, 6, BLK, 128), jnp.bfloat16)] * CHILDREN
+        scratch_shapes=[vmem((4, 6, BLK, 128), jnp.bfloat16)] * (2 * CHILDREN)
         + [
             vmem((UNITS, BLK, 2 * BLK), jnp.bfloat16),
             vmem((BLK, BLK), jnp.bfloat16),

time: 47.3 us -> 47.3 us (level)
  no operation moved by 1% of the time
where the time goes in v7:
time: 47.3 us; the launch traced here: 47.2 us
  Pallas kernels  46.6 us (99%)
  other arithmetic  0.58 us (1%)
    pallas_call x1, Pallas kernels, per_device(): pl.pallas_call(kernel, out_shape=vmem((8, 128), jnp.float32), in_specs=[p...  46.6 us

profile of v7, /device:TPU:1, one launch (start us, length us, event | category | flops | bytes accessed | tf_op | source)
XLA Modules:
  0.0 47.2 jit_solution(6970738335575054816)
XLA Ops:
  0.0 0.0 copy-start
  0.0 46.6 %shard_map.46 = f32[8,128]{1,0:T(8,128)S(1)} custom-call(s32[3,24]{1,0:T(4,128)} %anc_hbm.1, bf16[512,1024]{1,0:T(8,128)(2,1)} %root.1, bf16[3,3,256,128]{3,2,1,0:T(8,128)(2,1)} %bitcast.1), custom_call_target="tpu_custom_call" | custom-call | tf_op jit(solution)/shard_map/pallas_call | solution.py:434
  46.6 0.0 copy-done
  46.6 0.6 %slice_add_fusion = f32[3,128]{1,0:T(4,128)} fusion(f32[3,128]{1,0:T(4,128)S(1)} %copy-done, f32[8,128]{1,0:T(8,128)S(1)} %shard_map.46), kind=kLoop, calls=%fused_computation | loop fusion | flops 384 | bytes 4608 | tf_op jit(solution)/shard_map/add | solution.py:468
Async XLA Ops:
  0.0 46.6 %copy-start = (f32[3,128]{1,0:T(4,128)S(1)}, f32[3,128]{1,0:T(4,128)}, u32[]{:S(2)}) copy-start(f32[3,128]{1,0:T(4,128)} %param.7) | copy-start | bytes 4612

commit v8 on v7

--- a/solution.py
+++ b/solution.py
@@ -15,10 +15,10 @@
 SOURCES = ((0, 0), (0, 1), (1, 0), (3, 0), (1, 1), (3, 1), (2, 0), (2, 1))
 UNITS = 2 * len(SOURCES)
 ORDER = (
-    ("bd1", "bu1", "rb1u", "rb0u", "a0", "bd0", "a2", "rb0d", "bu0", "ra0", "ra1", "eu1", "cd0"),
-    ("rb1d", "a1", "du1", "bu2", "bd2", "ed1", "near", "rc0u", "rc0d", "dd1", "du0", "re1d", "rd1u"),
-    ("cu0", "do0", "rd1d", "cd2", "re1u", "opposite", "ef1", "ks2", "rd0d", "rd0u", "ka0", "du2", "re1f"),
-    ("ka1", "dd2", "eu2", "cu2", "ed2", "kb0", "do2", "kb1", "ef2", "ka2", "m0:8:12", "ku2", "m0:12:14"),
+    ("bd1", "bu1", "rb1u", "bd0", "rb0u", "a0", "a2", "rb0d", "bu0", "ra0", "ra1", "eu1", "cd0"),
+    ("rb1d", "near", "a1", "du1", "bu2", "bd2", "rc0u", "rd1u", "ed1", "rc0d", "dd1", "du0", "re1d"),
+    ("cu0", "do0", "rd1d", "cd2", "opposite", "re1u", "du2", "ef1", "ks2", "rd0d", "rd0u", "ka0", "cu2"),
+    ("re1f", "ka1", "eu2", "dd2", "ed2", "kb0", "do2", "kb1", "ef2", "ka2", "m0:8:12", "ku2", "m0:12:14"),
     ("m0:0:8", "m1:12:14", "m1:8:12", "kd2", "kf2", "m1:14:16", "m1:0:8", "m0:14:16", "m2:8:14", "m2:0:8", "m2:14:16"),
 )
 ORDER = sum(ORDER, ())

time: 47.3 us -> 47.3 us (level)
  no operation moved by 1% of the time
where the time goes in v8:
time: 47.3 us; the launch traced here: 47.2 us
  Pallas kernels  46.6 us (99%)
  other arithmetic  0.58 us (1%)
    pallas_call x1, Pallas kernels, per_device(): pl.pallas_call(kernel, out_shape=vmem((8, 128), jnp.float32), in_specs=[p...  46.6 us

profile of v8, /device:TPU:1, one launch (start us, length us, event | category | flops | bytes accessed | tf_op | source)
XLA Modules:
  0.0 47.2 jit_solution(3701401416173674272)
XLA Ops:
  0.0 0.0 copy-start
  0.0 46.6 %shard_map.46 = f32[8,128]{1,0:T(8,128)S(1)} custom-call(s32[3,24]{1,0:T(4,128)} %anc_hbm.1, bf16[512,1024]{1,0:T(8,128)(2,1)} %root.1, bf16[3,3,256,128]{3,2,1,0:T(8,128)(2,1)} %bitcast.1), custom_call_target="tpu_custom_call" | custom-call | tf_op jit(solution)/shard_map/pallas_call | solution.py:434
  46.6 0.0 copy-done
  46.6 0.6 %slice_add_fusion = f32[3,128]{1,0:T(4,128)} fusion(f32[3,128]{1,0:T(4,128)S(1)} %copy-done, f32[8,128]{1,0:T(8,128)S(1)} %shard_map.46), kind=kLoop, calls=%fused_computation | loop fusion | flops 384 | bytes 4608 | tf_op jit(solution)/shard_map/add | solution.py:468
Async XLA Ops:
  0.0 46.6 %copy-start = (f32[3,128]{1,0:T(4,128)S(1)}, f32[3,128]{1,0:T(4,128)}, u32[]{:S(2)}) copy-start(f32[3,128]{1,0:T(4,128)} %param.7) | copy-start | bytes 4612
